TPU v7x, 256 devices: a whole 4x4x8 slice. The times are simulated.
256 devices in a mesh: cfg: 2 (over core), fsdp: 8 (over x_hi, y), seq: 16 (over x_lo, z).
Axes of the slice: x: 4 (x_hi: 2, x_lo: 2; x = x_hi * 2 + x_lo), y: 4, z: 8, core: 2. Of those that a mesh axis runs over, the one named last changes fastest.
Arguments:
- query_act: bfloat16 [2, 8, 2048, 2048], P('cfg', 'fsdp', 'seq'), may hold values from -24 to 24
- key_act: bfloat16 [2, 8, 2048, 2048], P('cfg', 'fsdp', 'seq'), may hold values from -4 to 4
- value_act: bfloat16 [2, 8, 2048, 2048], P('cfg', 'fsdp', 'seq'), may hold values from -6 to 6
- out_weight: bfloat16 [2048, 1536], P(('fsdp', 'seq')), may hold values from -0.125 to 0.125
- reward_dir: bfloat16 [8, 2048, 1536], P('fsdp', 'seq'), may hold values from -6 to 6
- guide_index: int32 [1], replicated, may hold values from 0 to 127
- step_index: int32 [1], replicated, may hold values from 0 to 49
Outputs:
- guided: bfloat16 [8, 2048, 1536], P('fsdp', 'seq')
- grad_query: bfloat16 [2, 8, 2048, 2048], P('cfg', 'fsdp', 'seq')
- grad_key: bfloat16 [2, 8, 2048, 2048], P('cfg', 'fsdp', 'seq')
- grad_value: bfloat16 [2, 8, 2048, 2048], P('cfg', 'fsdp', 'seq')
- grad_weight: float32 [2048, 1536], P(('fsdp', 'seq'))
All inputs are finite; a program needn't handle non-finite values.
Results may differ from a plain program's by a relative error of at most 0.01.
Values may be sent and summed in bfloat16 or wider, within the bound.
No kernel may reach another device: no remote copies, remote signals or barrier semaphores. Data moves between devices by JAX's collectives and lax.ppermute only.
A program may use at most 128 MiB of HBM per device.

v0:
```python
import functools

import jax
import jax.numpy as jnp
from jax import lax
from jax.experimental import pallas as pl
from jax.experimental.pallas import tpu as pltpu
from jax.sharding import PartitionSpec as P

HDIM = 128
STEPS = 50
GUIDE_STEP = 0.04
LOG2E = 1.4426950408889634
BF = jnp.bfloat16
F32 = jnp.float32
NT = (((1,), (1,)), ((), ()))
VMEM_LIMIT = 20 * 1024 * 1024


def params():
    return pltpu.CompilerParams(vmem_limit_bytes=VMEM_LIMIT)


def whole(count):
    return [pl.BlockSpec(memory_space=pltpu.VMEM) for _ in range(count)]


def anywhere():
    return pl.BlockSpec(memory_space=pl.ANY)


def full(array):
    rank = len(array.shape)
    return pl.BlockSpec(array.shape, lambda i: (0,) * rank)


def scalars_spec():
    return pl.BlockSpec(memory_space=pltpu.SMEM)


def call(kernel, name, out_shape, in_specs, out_specs=None, flops=1, **kwargs):
    if out_specs is None:
        out_specs = whole(len(out_shape)) if isinstance(out_shape, tuple) else whole(1)[0]
    return pl.pallas_call(
        kernel,
        out_shape=out_shape,
        in_specs=in_specs,
        out_specs=tuple(out_specs) if isinstance(out_shape, tuple) else out_specs,
        compiler_params=params(),
        cost_estimate=pl.CostEstimate(flops=flops, bytes_accessed=1, transcendentals=0),
        name=name,
        **kwargs,
    )


def shaped(shape, dtype=BF):
    return jax.ShapeDtypeStruct(shape, dtype)


def kept(shape, dtype=BF):
    return pltpu.VMEM(shape, dtype)


def pin(array):
    return pltpu.with_memory_space_constraint(array, pltpu.VMEM)


def spilled(shape, dtype=BF):
    return pltpu.HBM(shape, dtype)


def out(array):
    return pltpu.with_memory_space_constraint(array, pltpu.HBM)


def ordered(orders):
    return [anywhere()] * len(orders)


def lanes_of(head):
    return slice(head * HDIM, (head + 1) * HDIM)


def pack_kernel(*refs):
    in_refs, out_ref = refs[:-1], refs[-1]
    rows = in_refs[0].shape[0]
    for head in range(out_ref.shape[0]):
        for place, ref in enumerate(in_refs):
            out_ref[head, place * rows : (place + 1) * rows, :] = ref[:, lanes_of(head)]


def pack_heads(*arrays):
    rows, width = arrays[0].shape
    return call(
        pack_kernel,
        "pack_heads",
        kept((width // HDIM, len(arrays) * rows, HDIM)),
        [full(array) for array in arrays],
        grid=(1,),
    )(*[out(array) for array in arrays])


def unpack_kernel(in_ref, *out_refs):
    rows = out_refs[0].shape[0]
    for head in range(in_ref.shape[0]):
        for place, ref in enumerate(out_refs):
            ref[:, lanes_of(head)] = in_ref[head, place * rows : (place + 1) * rows, :]


def unpack_heads(packed, count):
    target = shaped((packed.shape[1] // count, packed.shape[0] * HDIM))
    return call(
        unpack_kernel,
        "unpack_heads",
        (target,) * count,
        [full(packed)],
        [full(target)] * count,
        grid=(1,),
    )(packed)


CHUNK = 512


def forward_kernel(qkv_ref, *refs):
    out_ref, probs_ref, held, sems = refs[-4:]
    shards, total_rows, _ = qkv_ref.shape
    rows = total_rows // 3
    length = shards * rows
    keys = qkv_ref[:, rows : 2 * rows, :].reshape(length, HDIM)
    value_t = qkv_ref[:, 2 * rows :, :].reshape(length, HDIM).astype(F32).T.astype(BF)
    scale = HDIM ** (-0.5) * LOG2E
    take = CHUNK // rows
    copies = []
    for part in range(length // CHUNK):
        here = slice(part * take, (part + 1) * take)
        query = qkv_ref[here, :rows, :].reshape(CHUNK, HDIM)
        scores = lax.dot_general(keys, query, NT, preferred_element_type=F32)
        peak = jnp.max(scores, axis=0, keepdims=True) * scale
        weights = jnp.exp2(scores * scale - peak)
        total = jnp.sum(weights, axis=0, keepdims=True)
        probs = (weights * (1.0 / total)).astype(BF)
        lanes = pl.ds(part * CHUNK, CHUNK)
        held[:, lanes] = probs
        copy = pltpu.make_async_copy(held.at[:, lanes], probs_ref.at[:, lanes], sems.at[part])
        copy.start()
        copies.append(copy)
        mixed_t = jnp.dot(value_t, probs, preferred_element_type=F32)
        out_ref[here] = mixed_t.T.astype(BF).reshape(take, rows, HDIM)
    for copy in copies:
        copy.wait()


def attend_forward(qkv, *orders):
    shards, total_rows, _ = qkv.shape
    rows = total_rows // 3
    length = shards * rows
    return call(
        forward_kernel,
        "attend_forward",
        (kept((shards, rows, HDIM)), spilled((length, length))),
        whole(1) + ordered(orders),
        whole(1) + [anywhere()],
        scratch_shapes=[
            pltpu.VMEM((length, length), BF),
            pltpu.SemaphoreType.DMA((length // CHUNK,)),
        ],
    )(qkv, *[order if order.ndim == 1 else out(order) for order in orders])


def backward_kernel(qkv_ref, mixed_ref, grad_ref, probs_ref, *refs):
    out_ref, query_t, inner, held, sems = refs[-5:]
    shards, rows, _ = mixed_ref.shape
    length = shards * rows
    factor = HDIM ** (-0.5)
    chunk = CHUNK // 2
    take = chunk // rows

    def fetch(part):
        span = pl.ds(pl.multiple_of(part * CHUNK, CHUNK), CHUNK)
        return pltpu.make_async_copy(probs_ref.at[span], held.at[span], sems.at[part])

    for part in range(length // CHUNK):
        fetch(part).start()
    product = grad_ref[...].astype(F32) * mixed_ref[...].astype(F32)
    inner[...] = jnp.sum(product.reshape(length, HDIM).T, axis=0, keepdims=True)
    query_t[...] = jnp.zeros_like(query_t)

    def one_chunk(part):
        here = pl.ds(part * take, take)
        grad = grad_ref[...].reshape(length, HDIM)
        query = qkv_ref[:, :rows, :].reshape(length, HDIM)
        probs = held[pl.ds(pl.multiple_of(part * chunk, chunk), chunk), :]
        keys = qkv_ref[here, rows : 2 * rows, :].reshape(chunk, HDIM)
        value = qkv_ref[here, 2 * rows :, :].reshape(chunk, HDIM)
        grad_value = jnp.dot(probs, grad, preferred_element_type=F32)
        out_ref[here, 2 * rows :, :] = grad_value.astype(BF).reshape(take, rows, HDIM)
        grad_probs = lax.dot_general(value, grad, NT, preferred_element_type=F32)
        grad_scores = (probs.astype(F32) * (grad_probs - inner[...])).astype(BF)
        grad_key = jnp.dot(grad_scores, query, preferred_element_type=F32) * factor
        out_ref[here, rows : 2 * rows, :] = grad_key.astype(BF).reshape(take, rows, HDIM)
        query_t[...] += jnp.dot(keys.T, grad_scores, preferred_element_type=F32)

    @pl.loop(0, length // CHUNK)
    def _(part):
        fetch(part).wait()
        one_chunk(2 * part)
        one_chunk(2 * part + 1)

    grad_query = (query_t[...] * factor).T.astype(BF)
    out_ref[:, :rows, :] = grad_query.reshape(shards, rows, HDIM)


def attend_backward(qkv, mixed, grad, probs, *orders):
    length = probs.shape[0]
    return call(
        backward_kernel,
        "attend_backward",
        kept(qkv.shape),
        [full(qkv), full(mixed), full(grad), anywhere()] + ordered(orders),
        whole(1)[0],
        grid=(1,),
        flops=16 * length * length * HDIM,
        scratch_shapes=[
            pltpu.VMEM((HDIM, length), F32),
            pltpu.VMEM((1, length), F32),
            pltpu.VMEM((length, length), BF),
            pltpu.SemaphoreType.DMA((length // CHUNK,)),
        ],
    )(out(qkv), out(mixed), grad, out(probs), *[out(order) for order in orders])


def head_of(place_ref, dx, dy):
    return place_ref[1 + 4 * dy + dx]


def head_of(place_ref, dx, dy):
    return place_ref[1 + 4 * dy + dx]


def assemble_kernel(place_ref, *refs):
    groups, out_ref = refs[:-2], refs[-1]
    deep = groups[0].shape[1]
    for dy, (one, two) in enumerate(zip(groups[:4], groups[4:])):
        for dx in range(4):
            start = pl.multiple_of(head_of(place_ref, dx, dy) * deep, deep)
            out_ref[pl.ds(start, deep), :] = (one if dx < 2 else two)[dx % 2]


def assemble(place, groups, order):
    _, deep, wide = groups[0].shape
    return call(
        assemble_kernel,
        "assemble",
        kept((16 * deep, wide)),
        [scalars_spec()] + [full(group) for group in groups] + [anywhere()],
        whole(1)[0],
        grid=(1,),
        flops=10000000000,
    )(place, *[group if i % 4 == 2 else out(group) for i, group in enumerate(groups)], order)


def project_kernel(
    place_ref, scalar_ref, own_ref, other_ref, reward_ref, weight_ref,
    guided_ref, grad_ref, keep_ref, send_ref,
):
    rows = own_ref.shape[1]
    half = guided_ref.shape[1]
    heads = own_ref.shape[0]
    blocks = heads // 2
    deep = 2 * HDIM
    first = place_ref[0] == 0
    gate, strength = scalar_ref[0], scalar_ref[1]
    total = None
    for block in range(blocks):
        head = 2 * block
        columns = jnp.concatenate(
            [
                jnp.concatenate([own_ref[head], own_ref[head + 1]], axis=1),
                jnp.concatenate([other_ref[head], other_ref[head + 1]], axis=1),
            ],
            axis=0,
        )
        part = jnp.dot(
            columns, weight_ref[block * deep : (block + 1) * deep], preferred_element_type=F32
        )
        total = part if total is None else total + part
    branch_out = (gate * total).astype(BF).astype(F32)
    own_out, other_out = branch_out[:rows], branch_out[rows:]
    cond = jnp.where(first, own_out, other_out)
    uncond = jnp.where(first, other_out, own_out)
    guided = uncond + strength * (cond - uncond)
    guided_ref[...] = guided.astype(BF)
    reward = jnp.where(first, reward_ref[:, :half], reward_ref[:, half:]).astype(F32)
    resid = reward - guided
    own_coeff = gate * jnp.where(first, strength, 1.0 - strength)
    other_coeff = gate * jnp.where(first, 1.0 - strength, strength)
    grad = jnp.concatenate([own_coeff * resid, other_coeff * resid], axis=0).astype(BF)
    grad_ref[...] = grad
    for block in range(blocks):
        part = lax.dot_general(
            grad, weight_ref[block * deep : (block + 1) * deep], NT, preferred_element_type=F32
        )
        for odd in range(2):
            lanes = part[:, lanes_of(odd)]
            keep_ref[2 * block + odd] = lanes[:rows]
            send_ref[2 * block + odd] = lanes[rows:].astype(BF)


def project(place, scalars, own, other, reward, weight):
    heads, rows, _ = own.shape
    half = reward.shape[1] // 2
    return call(
        project_kernel,
        "project",
        (
            spilled((rows, half)),
            kept((2 * rows, half)),
            kept((heads, rows, HDIM), F32),
            kept((heads, rows, HDIM)),
        ),
        [scalars_spec(), scalars_spec()] + whole(2) + [full(reward)] + whole(1),
        [pl.BlockSpec((rows, half), lambda i: (0, 0))] + whole(3),
        grid=(1,),
    )(place, scalars, pin(own), pin(other), out(reward), pin(weight))


def weight_kernel(place_ref, own_ref, other_ref, grad_ref, order_ref, *refs):
    grad = grad_ref[...]
    for dy, ref in enumerate(refs):
        for dx in range(4):
            head = head_of(place_ref, dx, dy)
            flipped = jnp.concatenate([own_ref[head].T, other_ref[head].T], axis=1)
            ref[dx] = jnp.dot(flipped, grad, preferred_element_type=F32).astype(BF)


def weight_gradient(place, own, other, grad, order):
    group = spilled((4, HDIM, grad.shape[1]))
    return call(
        weight_kernel,
        "weight_gradient",
        (group,) * 4,
        [scalars_spec()] + whole(3) + [anywhere()],
        [full(group)] * 4,
        grid=(1,),
    )(place, pin(own), pin(other), pin(grad), order)


def add_kernel(keep_ref, got_ref, out_ref):
    out_ref[...] = (keep_ref[...] + got_ref[...].astype(F32)).astype(BF)


def add_after(keep, got):
    return call(add_kernel, "add_after", kept(got.shape), whole(2))(pin(keep), pin(got))


def halves_kernel(place_ref, *refs):
    arrays, keep_ref, send_ref, held = refs[:4], refs[-3], refs[-2], refs[-1]
    rows = keep_ref.shape[0]
    held[...] = sum(ref[...].astype(F32) for ref in arrays)
    start = pl.multiple_of((place_ref[17] >> 2) * rows, rows)
    other = pl.multiple_of(rows - start, rows)
    keep_ref[...] = held[pl.ds(start, rows), :]
    send_ref[...] = held[pl.ds(other, rows), :].astype(BF)


def z_halves(place, arrays, order):
    rows, wide = arrays[0].shape
    outs = (spilled((rows // 2, wide), F32), spilled((rows // 2, wide)))
    return call(
        halves_kernel,
        "z_halves",
        outs,
        [scalars_spec()] + [full(array) for array in arrays] + [anywhere()],
        [full(target) for target in outs],
        grid=(1,),
        flops=10000000000,
        scratch_shapes=[pltpu.VMEM((rows, wide), F32)],
    )(place, *[out(array) for array in arrays], out(order))


def quarters_kernel(place_ref, keep_ref, got_ref, *refs):
    out_refs, held = refs[:-1], refs[-1]
    deep = out_refs[0].shape[0]
    held[...] = keep_ref[...] + got_ref[...].astype(F32)
    for step, ref in enumerate(out_refs):
        start = pl.multiple_of(((place_ref[17] + step) & 3) * deep, deep)
        ref[...] = held[pl.ds(start, deep), :].astype(ref.dtype)


def z_quarters(place, keep, got):
    rows, wide = keep.shape
    target = (rows // 4, wide)
    return call(
        quarters_kernel,
        "z_quarters",
        (kept(target, F32),) + (kept(target),) * 3,
        [scalars_spec(), full(keep), full(got)],
        whole(4),
        grid=(1,),
        scratch_shapes=[pltpu.VMEM((rows, wide), F32)],
    )(place, keep, got)


def total_kernel(*refs):
    in_refs, out_ref = refs[:-1], refs[-1]
    out_ref[...] = sum(ref[...].astype(F32) for ref in in_refs)


def total_of(arrays):
    return call(
        total_kernel,
        "total_of",
        kept(arrays[0].shape, F32),
        whole(len(arrays)),
        whole(1)[0],
    )(*[pin(array) for array in arrays])


def swap_cfg(value):
    return lax.ppermute(value, "cfg", [(0, 1), (1, 0)])


def shift_y(value, step):
    pairs = [(i, (i // 4) * 4 + (i % 4 + step) % 4) for i in range(8)]
    return lax.ppermute(value, "fsdp", pairs)


def shift_x(value, step):
    pairs = []
    for fsdp in range(8):
        for seq in range(16):
            x = ((fsdp // 4) * 2 + seq // 8 + step) % 4
            target = ((x // 2) * 4 + fsdp % 4) * 16 + (x % 2) * 8 + seq % 8
            pairs.append((fsdp * 16 + seq, target))
    return lax.ppermute(value, ("fsdp", "seq"), pairs)


def gather_groups(piece):
    right, left, far = shift_x(piece, -1), shift_x(piece, 1), shift_x(piece, 2)
    near = jnp.stack([piece, right])
    past = jnp.stack([far, left])
    near_left, near_right = shift_y(near, 1), shift_y(near, -1)
    past_left, past_right = shift_y(past, 1), shift_y(past, -1)
    near_far = shift_y(near_left, 1)
    past_far = shift_y(past_right, -1)
    return (near, near_right, near_far, near_left, past, past_right, past_far, past_left)


def group_kernel(*refs):
    in_refs, out_refs = refs[:4], refs[5:]
    for slot, target in enumerate(out_refs):
        total = sum(ref[slot].astype(F32) for ref in in_refs)
        target[...] = total.astype(target.dtype)


def group_sums(groups, order):
    shape = groups[0].shape[1:]
    outs = (spilled(shape, F32),) + (spilled(shape),) * 3
    return call(
        group_kernel,
        "group_sums",
        outs,
        [full(group) for group in groups] + [anywhere()],
        [full(target) for target in outs],
        grid=(1,),
        flops=10000000000,
    )(*[out(group) for group in groups], out(order))


def scatter_first(groups):
    return [groups[0]] + [shift_y(groups[step], step) for step in range(1, 4)]


def scatter_rest(place, groups, order, packed):
    sums = group_sums(groups, packed)
    ring = [sums[0]] + [shift_x(sums[step], step) for step in range(1, 4)]
    keep, send = z_halves(place, ring, order)
    got = lax.ppermute(send, "seq", [(i, i ^ 4) for i in range(16)])
    parts = list(z_quarters(place, keep, got))
    for step in range(1, 4):
        pairs = [(i, (i & 12) + ((i + step) & 3)) for i in range(16)]
        parts[step] = lax.ppermute(parts[step], "seq", pairs)
    return total_of(parts)


def over_seq(array):
    return lax.all_to_all(array, "seq", split_axis=0, concat_axis=0, tiled=True)


def over_z(array):
    groups = [list(range(8)), list(range(8, 16))]
    return lax.all_to_all(
        array, "seq", split_axis=0, concat_axis=0, axis_index_groups=groups, tiled=True
    )


def join_kernel(place_ref, own_ref, other_ref, order_ref, out_ref):
    first = place_ref[0] == 0
    half = own_ref.shape[1]
    out_ref[:, :half] = jnp.where(first, own_ref[...], other_ref[...])
    out_ref[:, half:] = jnp.where(first, other_ref[...], own_ref[...])


def joined(place, own, other, order, where=out):
    rows, half = own.shape
    return call(
        join_kernel,
        "joined",
        shaped((rows, 2 * half), own.dtype),
        [scalars_spec(), full(own), full(other), anywhere()],
        pl.BlockSpec((rows, 2 * half), lambda i: (0, 0)),
        grid=(1,),
    )(place, where(own), where(other), out(order))


def places():
    cfg = lax.axis_index("cfg")
    fsdp = lax.axis_index("fsdp")
    x = (fsdp >> 2) * 2 + (lax.axis_index("seq") >> 3)
    y = fsdp & 3
    slots = jnp.arange(16)
    there = (x + (slots & 3)) & 3
    block = (there >> 1) * 4 + ((y + (slots >> 2)) & 3)
    table = 2 * block + (there & 1)
    return jnp.concatenate([cfg[None], table, (lax.axis_index("seq") & 7)[None]]).astype(jnp.int32)


def local(query_act, key_act, value_act, out_weight, reward_dir, guide_index, step_index):
    place = places()
    moment = step_index[0].astype(F32)
    gate = jnp.cos(0.5 * jnp.pi * (moment + 0.5) / STEPS)
    strength = 1.0 + GUIDE_STEP * guide_index[0].astype(F32)
    scalars = jnp.stack([gate, strength])
    half = out_weight.shape[1] // 2
    own_half = jnp.where(place[0] == 0, out_weight[:, :half], out_weight[:, half:])
    piece = over_z(jnp.broadcast_to(own_half[None], (8,) + own_half.shape)).reshape(-1, half)
    groups = gather_groups(piece)
    qkv = over_seq(pack_heads(query_act[0, 0], key_act[0, 0], value_act[0, 0]))
    mixed_h, probs = attend_forward(qkv, groups[1], groups[3], groups[5], groups[7], place, scalars)
    mixed = over_seq(mixed_h)
    weight = assemble(place, groups, mixed)
    mixed_other = swap_cfg(mixed)
    guided, grad_out, keep, send = project(
        place, scalars, mixed, mixed_other, reward_dir[0], weight
    )
    grad_mixed = add_after(keep, swap_cfg(send))
    parts = weight_gradient(place, mixed, mixed_other, grad_out, grad_mixed)
    grad_h = over_seq(grad_mixed)
    parts = scatter_first(parts)
    packed = attend_backward(qkv, mixed_h, grad_h, probs, parts[0])
    guided_all = joined(place, guided, swap_cfg(guided), packed)
    last = over_seq(packed)
    grad_half = scatter_rest(place, parts, guided_all, packed)
    grad_query, grad_key, grad_value = unpack_heads(last, 3)
    grad_weight = joined(place, grad_half, swap_cfg(grad_half), grad_query, pin)
    return (
        guided_all[None],
        grad_query[None, None],
        grad_key[None, None],
        grad_value[None, None],
        grad_weight,
    )


def solution(mesh):
    placed = (
        P("cfg", "fsdp", "seq", None),
        P("cfg", "fsdp", "seq", None),
        P("cfg", "fsdp", "seq", None),
        P(("fsdp", "seq"), None),
        P("fsdp", "seq", None),
        P(),
        P(),
    )
    return jax.shard_map(
        local,
        mesh=mesh,
        in_specs=placed,
        out_specs=(
            P("fsdp", "seq", None),
            P("cfg", "fsdp", "seq", None),
            P("cfg", "fsdp", "seq", None),
            P("cfg", "fsdp", "seq", None),
            P(("fsdp", "seq"), None),
        ),
        check_vma=False,
    )
```

profile of v0, /device:TPU:1, one launch (start us, length us, event | category | flops | bytes accessed | tf_op | source)
XLA Modules:
  0.0 195.9 jit_solution(2844386775596594343)
XLA Ops:
  2.1 9.0 %all-to-all-start.1 = ((bf16[8,16,768]{2,1,0:T(8,128)(2,1)}), bf16[8,16,768]{2,1,0:T(8,128)(2,1)S(1)}, u32[]{:S(2)}, u32[]{:S(2)}) async-start(bf16[8,16,768]{2,1,0:T(8,128)(2,1)} %broadcast_in_dim.26), calls=%async_computation.1 | async-start | bytes 393216 | tf_op jit(solution)/shard_map/all_to_all | solution.py:493
  11.1 2.8 %pack_heads.1 = bf16[16,384,128]{2,1,0:T(8,128)(2,1)} custom-call(bf16[128,2048]{1,0:T(8,128)(2,1)} %bitcast.20, bf16[128,2048]{1,0:T(8,128)(2,1)} %bitcast.21, bf16[128,2048]{1,0:T(8,128)(2,1)} %bitcast.22), custom_call_target="tpu_custom_call" | custom-call | flops 1 | bytes 1 | tf_op jit(solution)/shard_map/pack_heads/pallas_call | solution.py:94
  13.9 6.0 %all-to-all-done.1 = bf16[8,16,768]{2,1,0:T(8,128)(2,1)S(1)} async-done(((bf16[8,16,768]{2,1,0:T(8,128)(2,1)}), bf16[8,16,768]{2,1,0:T(8,128)(2,1)S(1)}, u32[]{:S(2)}, u32[]{:S(2)}) %all-to-all-start.1) | async-done | bytes 196640 | tf_op jit(solution)/shard_map/all_to_all | solution.py:493
  19.9 4.1 %all-to-all-start = ((bf16[16,384,128]{2,1,0:T(8,128)(2,1)}), bf16[16,384,128]{2,1,0:T(8,128)(2,1)S(1)}, u32[]{:S(2)}, u32[]{:S(2)}) async-start(bf16[16,384,128]{2,1,0:T(8,128)(2,1)} %pack_heads.1), calls=%async_computation | async-start | bytes 3145728 | tf_op jit(solution)/shard_map/all_to_all | solution.py:488
  24.0 2.6 %collective-permute-start = (bf16[128,768]{1,0:T(8,128)(2,1)S(1)}, bf16[128,768]{1,0:T(8,128)(2,1)S(1)}, u32[]{:S(2)}, u32[]{:S(2)}) collective-permute-start(bf16[128,768]{1,0:T(8,128)(2,1)S(1)} %bitcast.15), channel_id=1, source_target_pairs={{0,72},{1,73},{2,74},{3,75},{4,76},{5,77},{6,78},{7,79},{8,0},{9,1... | collective-permute-start | bytes 589832 | tf_op jit(solution)/shard_map/ppermute | solution.py:436
  28.0 7.2 %collective-permute-done = bf16[128,768]{1,0:T(8,128)(2,1)S(1)} collective-permute-done((bf16[128,768]{1,0:T(8,128)(2,1)S(1)}, bf16[128,768]{1,0:T(8,128)(2,1)S(1)}, u32[]{:S(2)}, u32[]{:S(2)}) %collective-permute-start) | collective-permute-done | bytes 196640 | tf_op jit(solution)/shard_map/ppermute | solution.py:436
  38.2 4.0 %collective-permute-done.3 = bf16[128,768]{1,0:T(8,128)(2,1)S(1)} collective-permute-done((bf16[128,768]{1,0:T(8,128)(2,1)S(1)}, bf16[128,768]{1,0:T(8,128)(2,1)S(1)}, u32[]{:S(2)}, u32[]{:S(2)}) %collective-permute-start.3) | collective-permute-done | bytes 196640 | tf_op jit(solution)/shard_map/ppermute | solution.py:436
  46.9 7.8 %collective-permute-done.6.refs_3_.refs_7_ = bf16[2,128,768]{2,1,0:T(8,128)(2,1)S(1)} collective-permute-done((bf16[2,128,768]{2,1,0:T(8,128)(2,1)S(1)}, bf16[2,128,768]{2,1,0:T(8,128)(2,1)S(1)}, u32[]{:S(2)}, u32[]{:S(2)}) %collective-permute-start.6) | collective-permute-done | bytes 393248 | tf_op jit(solution)/shard_map/ppermute | solution.py:426
  54.7 5.4 %all-to-all-done.qkv_ref = bf16[16,384,128]{2,1,0:T(8,128)(2,1)S(1)} async-done(((bf16[16,384,128]{2,1,0:T(8,128)(2,1)}), bf16[16,384,128]{2,1,0:T(8,128)(2,1)S(1)}, u32[]{:S(2)}, u32[]{:S(2)}) %all-to-all-start) | async-done | bytes 1572896 | tf_op jit(solution)/shard_map/all_to_all | solution.py:488
  60.1 9.6 %attend_forward.1 = (bf16[16,128,128]{2,1,0:T(8,128)(2,1)}, bf16[2048,2048]{1,0:T(8,128)(2,1)}) custom-call(bf16[16,384,128]{2,1,0:T(8,128)(2,1)S(1)} %all-to-all-done.qkv_ref, bf16[2,128,768]{2,1,0:T(8,128)(2,1)} %copy-done.5, bf16[2,128,768]{2,1,0:T(8,128)(2,1)} %copy-done.4, bf16[2,128,768]{2,1,0:T(8,128)(2,1)} %collective-permute-done.5.refs_2_.refs_5_, ...), custom_call_target="tpu_custom_call" | custom-call | flops 1 | bytes 1 | tf_op jit(solution)/shard_map/attend_forward/pallas_call | solution.py:158
  69.8 6.4 %all-to-all-start.2 = ((bf16[16,128,128]{2,1,0:T(8,128)(2,1)}), bf16[16,128,128]{2,1,0:T(8,128)(2,1)S(1)}, u32[]{:S(2)}, u32[]{:S(2)}) async-start(bf16[16,128,128]{2,1,0:T(8,128)(2,1)} %get-tuple-element.28.mixed_ref), calls=%async_computation.2 | async-start | bytes 1048576 | tf_op jit(solution)/shard_map/all_to_all | solution.py:488
  79.1 9.9 %all-to-all-done.2.refs_8_.own_ref = bf16[16,128,128]{2,1,0:T(8,128)(2,1)S(1)} async-done(((bf16[16,128,128]{2,1,0:T(8,128)(2,1)}), bf16[16,128,128]{2,1,0:T(8,128)(2,1)S(1)}, u32[]{:S(2)}, u32[]{:S(2)}) %all-to-all-start.2) | async-done | bytes 524320 | tf_op jit(solution)/shard_map/all_to_all | solution.py:488
  88.9 3.6 %collective-permute-start.7 = (bf16[16,128,128]{2,1,0:T(8,128)(2,1)S(1)}, bf16[16,128,128]{2,1,0:T(8,128)(2,1)S(1)}, u32[]{:S(2)}, u32[]{:S(2)}) collective-permute-start(bf16[16,128,128]{2,1,0:T(8,128)(2,1)S(1)} %all-to-all-done.2.refs_8_.own_ref), channel_id=1, source_target_pairs={{0,128},{128,0},{1,129},{129,1},{2,130},{130,2},{3,131},{131,3},{4... | collective-permute-start | bytes 1572872 | tf_op jit(solution)/shard_map/ppermute | solution.py:421
  94.3 3.8 %project.1 = (bf16[128,768]{1,0:T(8,128)(2,1)}, bf16[256,768]{1,0:T(8,128)(2,1)S(1)}, f32[16,128,128]{2,1,0:T(8,128)S(1)}, bf16[16,128,128]{2,1,0:T(8,128)(2,1)S(1)}) custom-call(s32[18]{0:T(128)S(1)} %pad_add_fusion.refs_4_.place_ref, f32[2]{0:T(128)S(1)} %pad_maximum_fusion.2.refs_5_.scalar_ref, bf16[16,128,128]{2,1,0:T(8,128)(2,1)S(1)} %all-to-all-done.2.refs_8_.own_ref, ...), custom_call_target="tpu_custom_call" | custom-call | flops 1 | bytes 1 | tf_op jit(solution)/shard_map/project/pallas_call | solution.py:313
  101.0 4.6 %all-to-all-start.3 = ((bf16[16,128,128]{2,1,0:T(8,128)(2,1)}), bf16[16,128,128]{2,1,0:T(8,128)(2,1)S(1)}, u32[]{:S(2)}, u32[]{:S(2)}) async-start(bf16[16,128,128]{2,1,0:T(8,128)(2,1)} %add_after.1.order_ref), calls=%async_computation.3 | async-start | bytes 1048576 | tf_op jit(solution)/shard_map/all_to_all | solution.py:488
  105.6 2.9 %weight_gradient.1 = (bf16[4,128,768]{2,1,0:T(8,128)(2,1)}, bf16[4,128,768]{2,1,0:T(8,128)(2,1)}, bf16[4,128,768]{2,1,0:T(8,128)(2,1)}, bf16[4,128,768]{2,1,0:T(8,128)(2,1)}) custom-call(s32[18]{0:T(128)S(1)} %pad_add_fusion.refs_4_.place_ref, bf16[16,128,128]{2,1,0:T(8,128)(2,1)S(1)} %all-to-all-done.2.refs_8_.own_ref, ...), custom_call_target="tpu_custom_call" | custom-call | flops 1 | bytes 1 | tf_op jit(solution)/shard_map/weight_gradient/pallas_call | solution.py:339
  113.5 5.9 %all-to-all-done.3.grad_ref = bf16[16,128,128]{2,1,0:T(8,128)(2,1)S(1)} async-done(((bf16[16,128,128]{2,1,0:T(8,128)(2,1)}), bf16[16,128,128]{2,1,0:T(8,128)(2,1)S(1)}, u32[]{:S(2)}, u32[]{:S(2)}) %all-to-all-start.3) | async-done | bytes 524320 | tf_op jit(solution)/shard_map/all_to_all | solution.py:488
  119.4 12.9 %attend_backward.1.order_ref.refs_4_ = bf16[16,384,128]{2,1,0:T(8,128)(2,1)} custom-call(bf16[16,384,128]{2,1,0:T(8,128)(2,1)} %copy-done, bf16[16,128,128]{2,1,0:T(8,128)(2,1)} %get-tuple-element.28.mixed_ref, bf16[16,128,128]{2,1,0:T(8,128)(2,1)S(1)} %all-to-all-done.3.grad_ref, bf16[2048,2048]{1,0:T(8,128)(2,1)} %get-tuple-element.32.probs_ref, ...), custom_call_target="tpu_custom_call" | custom-call | flops 8589934592 | bytes 1 | tf_op jit(solution)/shard_map/attend_backward/pallas_call | solution.py:216
  132.3 6.8 %all-to-all-start.4 = ((bf16[16,384,128]{2,1,0:T(8,128)(2,1)}), bf16[16,384,128]{2,1,0:T(8,128)(2,1)S(1)}, u32[]{:S(2)}, u32[]{:S(2)}) async-start(bf16[16,384,128]{2,1,0:T(8,128)(2,1)} %attend_backward.1.order_ref.refs_4_), calls=%async_computation.4 | async-start | bytes 3145728 | tf_op jit(solution)/shard_map/all_to_all | solution.py:488
  140.0 6.7 %collective-permute-done.13.refs_2_ = bf16[4,128,768]{2,1,0:T(8,128)(2,1)S(1)} collective-permute-done((bf16[4,128,768]{2,1,0:T(8,128)(2,1)}, bf16[4,128,768]{2,1,0:T(8,128)(2,1)S(1)}, u32[]{:S(2)}, u32[]{:S(2)}) %collective-permute-start.13) | collective-permute-done | bytes 786464 | tf_op jit(solution)/shard_map/ppermute | solution.py:426
  147.6 2.9 %group_sums.1 = (f32[128,768]{1,0:T(8,128)}, bf16[128,768]{1,0:T(8,128)(2,1)}, bf16[128,768]{1,0:T(8,128)(2,1)}, bf16[128,768]{1,0:T(8,128)(2,1)}) custom-call(bf16[4,128,768]{2,1,0:T(8,128)(2,1)} %get-tuple-element.34.refs_0_, bf16[4,128,768]{2,1,0:T(8,128)(2,1)} %copy-done.9, bf16[4,128,768]{2,1,0:T(8,128)(2,1)} %copy-done.10, ...), custom_call_target="tpu_custom_call" | custom-call | flops 10000000000 | bytes 1 | tf_op jit(solution)/shard_map/group_sums/pallas_call | solution.py:460
  157.2 11.0 %collective-permute-done.16.refs_2_ = bf16[128,768]{1,0:T(8,128)(2,1)S(1)} collective-permute-done((bf16[128,768]{1,0:T(8,128)(2,1)}, bf16[128,768]{1,0:T(8,128)(2,1)S(1)}, u32[]{:S(2)}, u32[]{:S(2)}) %collective-permute-start.16) | collective-permute-done | bytes 196640 | tf_op jit(solution)/shard_map/ppermute | solution.py:436
  171.8 8.6 %collective-permute-done.18.got_ref = bf16[64,768]{1,0:T(8,128)(2,1)S(1)} collective-permute-done((bf16[64,768]{1,0:T(8,128)(2,1)}, bf16[64,768]{1,0:T(8,128)(2,1)S(1)}, u32[]{:S(2)}, u32[]{:S(2)}) %collective-permute-start.18) | collective-permute-done | bytes 98336 | tf_op jit(solution)/shard_map/ppermute | solution.py:479
  188.1 5.0 %collective-permute-start.22 = (f32[16,768]{1,0:T(8,128)S(1)}, f32[16,768]{1,0:T(8,128)S(1)}, u32[]{:S(2)}, u32[]{:S(2)}) collective-permute-start(f32[16,768]{1,0:T(8,128)S(1)} %total_of.1.own_ref), channel_id=1, source_target_pairs={{0,128},{128,0},{1,129},{129,1},{2,130},{130,2},{3,131},{131,3},{4... | collective-permute-start | bytes 147464 | tf_op jit(solution)/shard_map/ppermute | solution.py:421
  (81 shorter events, 44.2 us)
Async XLA Ops:
  2.1 17.8 %all-to-all-start.1 = ((bf16[8,16,768]{2,1,0:T(8,128)(2,1)}), bf16[8,16,768]{2,1,0:T(8,128)(2,1)S(1)}, u32[]{:S(2)}, u32[]{:S(2)}) async-start(bf16[8,16,768]{2,1,0:T(8,128)(2,1)} %broadcast_in_dim.26), calls=%async_computation.1 | async-start | bytes 393216 | tf_op jit(solution)/shard_map/all_to_all | solution.py:493
  19.9 40.2 %all-to-all-start = ((bf16[16,384,128]{2,1,0:T(8,128)(2,1)}), bf16[16,384,128]{2,1,0:T(8,128)(2,1)S(1)}, u32[]{:S(2)}, u32[]{:S(2)}) async-start(bf16[16,384,128]{2,1,0:T(8,128)(2,1)} %pack_heads.1), calls=%async_computation | async-start | bytes 3145728 | tf_op jit(solution)/shard_map/all_to_all | solution.py:488
  24.0 11.2 %collective-permute-start = (bf16[128,768]{1,0:T(8,128)(2,1)S(1)}, bf16[128,768]{1,0:T(8,128)(2,1)S(1)}, u32[]{:S(2)}, u32[]{:S(2)}) collective-permute-start(bf16[128,768]{1,0:T(8,128)(2,1)S(1)} %bitcast.15), channel_id=1, source_target_pairs={{0,72},{1,73},{2,74},{3,75},{4,76},{5,77},{6,78},{7,79},{8,0},{9,1... | collective-permute-start | bytes 589832 | tf_op jit(solution)/shard_map/ppermute | solution.py:436
  26.7 11.5 %collective-permute-start.4 = (bf16[128,768]{1,0:T(8,128)(2,1)S(1)}, bf16[128,768]{1,0:T(8,128)(2,1)S(1)}, u32[]{:S(2)}, u32[]{:S(2)}) collective-permute-start(bf16[128,768]{1,0:T(8,128)(2,1)S(1)} %bitcast.16), channel_id=1, source_target_pairs={{0,8},{1,9},{2,10},{3,11},{4,12},{5,13},{6,14},{7,15},{8,64},{9,65... | collective-permute-start | bytes 589832 | tf_op jit(solution)/shard_map/ppermute | solution.py:436
  26.7 15.5 %collective-permute-start.3 = (bf16[128,768]{1,0:T(8,128)(2,1)S(1)}, bf16[128,768]{1,0:T(8,128)(2,1)S(1)}, u32[]{:S(2)}, u32[]{:S(2)}) collective-permute-start(bf16[128,768]{1,0:T(8,128)(2,1)S(1)} %bitcast.17), channel_id=1, source_target_pairs={{0,64},{1,65},{2,66},{3,67},{4,68},{5,69},{6,70},{7,71},{8,72},{9,... | collective-permute-start | bytes 589832 | tf_op jit(solution)/shard_map/ppermute | solution.py:436
  35.3 11.6 %collective-permute-start.2 = (bf16[2,128,768]{2,1,0:T(8,128)(2,1)S(1)}, bf16[2,128,768]{2,1,0:T(8,128)(2,1)S(1)}, u32[]{:S(2)}, u32[]{:S(2)}) collective-permute-start(bf16[2,128,768]{2,1,0:T(8,128)(2,1)S(1)} %pad_maximum_fusion.refs_0_), channel_id=1, source_target_pairs={{0,16},{16,32},{32,48},{48,0},{64,80},{80,96},{96,112},{112,64},{1... | collective-permute-start | bytes 1179656 | tf_op jit(solution)/shard_map/ppermute | solution.py:426
  36.6 10.2 %collective-permute-start.1 = (bf16[2,128,768]{2,1,0:T(8,128)(2,1)S(1)}, bf16[2,128,768]{2,1,0:T(8,128)(2,1)S(1)}, u32[]{:S(2)}, u32[]{:S(2)}) collective-permute-start(bf16[2,128,768]{2,1,0:T(8,128)(2,1)S(1)} %pad_maximum_fusion.refs_0_), channel_id=1, source_target_pairs={{0,48},{16,0},{32,16},{48,32},{64,112},{80,64},{96,80},{112,96},{1... | collective-permute-start | bytes 1179656 | tf_op jit(solution)/shard_map/ppermute | solution.py:426
  42.2 12.5 %collective-permute-start.6 = (bf16[2,128,768]{2,1,0:T(8,128)(2,1)S(1)}, bf16[2,128,768]{2,1,0:T(8,128)(2,1)S(1)}, u32[]{:S(2)}, u32[]{:S(2)}) collective-permute-start(bf16[2,128,768]{2,1,0:T(8,128)(2,1)S(1)} %pad_maximum_fusion.1.refs_4_), channel_id=1, source_target_pairs={{0,16},{16,32},{32,48},{48,0},{64,80},{80,96},{96,112},{112,64},{1... | collective-permute-start | bytes 1179656 | tf_op jit(solution)/shard_map/ppermute | solution.py:426
  43.6 11.2 %collective-permute-start.5 = (bf16[2,128,768]{2,1,0:T(8,128)(2,1)S(1)}, bf16[2,128,768]{2,1,0:T(8,128)(2,1)}, u32[]{:S(2)}, u32[]{:S(2)}) collective-permute-start(bf16[2,128,768]{2,1,0:T(8,128)(2,1)S(1)} %pad_maximum_fusion.1.refs_4_), channel_id=1, source_target_pairs={{0,48},{16,0},{32,16},{48,32},{64,112},{80,64},{96,80},{112,96},{1... | collective-permute-start | bytes 1179656 | tf_op jit(solution)/shard_map/ppermute | solution.py:426
  69.8 19.2 %all-to-all-start.2 = ((bf16[16,128,128]{2,1,0:T(8,128)(2,1)}), bf16[16,128,128]{2,1,0:T(8,128)(2,1)S(1)}, u32[]{:S(2)}, u32[]{:S(2)}) async-start(bf16[16,128,128]{2,1,0:T(8,128)(2,1)} %get-tuple-element.28.mixed_ref), calls=%async_computation.2 | async-start | bytes 1048576 | tf_op jit(solution)/shard_map/all_to_all | solution.py:488
  76.2 16.3 %collective-permute-start.8 = (bf16[2,128,768]{2,1,0:T(8,128)(2,1)}, bf16[2,128,768]{2,1,0:T(8,128)(2,1)S(1)}, u32[]{:S(2)}, u32[]{:S(2)}) collective-permute-start(bf16[2,128,768]{2,1,0:T(8,128)(2,1)} %copy-done.4), channel_id=1, source_target_pairs={{0,16},{16,32},{32,48},{48,0},{64,80},{80,96},{96,112},{112,64},{1... | collective-permute-start | bytes 1179656 | tf_op jit(solution)/shard_map/ppermute | solution.py:426
  77.6 15.0 %collective-permute-start.9 = (bf16[2,128,768]{2,1,0:T(8,128)(2,1)}, bf16[2,128,768]{2,1,0:T(8,128)(2,1)S(1)}, u32[]{:S(2)}, u32[]{:S(2)}) collective-permute-start(bf16[2,128,768]{2,1,0:T(8,128)(2,1)} %collective-permute-done.5.refs_2_.refs_5_), channel_id=1, source_target_pairs={{0,48},{16,0},{32,16},{48,32},{64,112},{80,64},{96,80},{112,96},{1... | collective-permute-start | bytes 1179656 | tf_op jit(solution)/shard_map/ppermute | solution.py:426
  88.9 5.4 %collective-permute-start.7 = (bf16[16,128,128]{2,1,0:T(8,128)(2,1)S(1)}, bf16[16,128,128]{2,1,0:T(8,128)(2,1)S(1)}, u32[]{:S(2)}, u32[]{:S(2)}) collective-permute-start(bf16[16,128,128]{2,1,0:T(8,128)(2,1)S(1)} %all-to-all-done.2.refs_8_.own_ref), channel_id=1, source_target_pairs={{0,128},{128,0},{1,129},{129,1},{2,130},{130,2},{3,131},{131,3},{4... | collective-permute-start | bytes 1572872 | tf_op jit(solution)/shard_map/ppermute | solution.py:421
  101.0 18.4 %all-to-all-start.3 = ((bf16[16,128,128]{2,1,0:T(8,128)(2,1)}), bf16[16,128,128]{2,1,0:T(8,128)(2,1)S(1)}, u32[]{:S(2)}, u32[]{:S(2)}) async-start(bf16[16,128,128]{2,1,0:T(8,128)(2,1)} %add_after.1.order_ref), calls=%async_computation.3 | async-start | bytes 1048576 | tf_op jit(solution)/shard_map/all_to_all | solution.py:488
  108.5 31.5 %collective-permute-start.12 = (bf16[4,128,768]{2,1,0:T(8,128)(2,1)}, bf16[4,128,768]{2,1,0:T(8,128)(2,1)S(1)}, u32[]{:S(2)}, u32[]{:S(2)}) collective-permute-start(bf16[4,128,768]{2,1,0:T(8,128)(2,1)} %get-tuple-element.38), channel_id=1, source_target_pairs={{0,16},{16,32},{32,48},{48,0},{64,80},{80,96},{96,112},{112,64},{1... | collective-permute-start | bytes 2359304 | tf_op jit(solution)/shard_map/ppermute | solution.py:426
  109.8 36.9 %collective-permute-start.13 = (bf16[4,128,768]{2,1,0:T(8,128)(2,1)}, bf16[4,128,768]{2,1,0:T(8,128)(2,1)S(1)}, u32[]{:S(2)}, u32[]{:S(2)}) collective-permute-start(bf16[4,128,768]{2,1,0:T(8,128)(2,1)} %get-tuple-element.39), channel_id=1, source_target_pairs={{0,32},{16,48},{32,0},{48,16},{64,96},{80,112},{96,64},{112,80},{1... | collective-permute-start | bytes 2359304 | tf_op jit(solution)/shard_map/ppermute | solution.py:426
  112.4 34.3 %collective-permute-start.14 = (bf16[4,128,768]{2,1,0:T(8,128)(2,1)}, bf16[4,128,768]{2,1,0:T(8,128)(2,1)}, u32[]{:S(2)}, u32[]{:S(2)}) collective-permute-start(bf16[4,128,768]{2,1,0:T(8,128)(2,1)} %get-tuple-element.40), channel_id=1, source_target_pairs={{0,48},{16,0},{32,16},{48,32},{64,112},{80,64},{96,80},{112,96},{1... | collective-permute-start | bytes 2359304 | tf_op jit(solution)/shard_map/ppermute | solution.py:426
  132.3 60.8 %all-to-all-start.4 = ((bf16[16,384,128]{2,1,0:T(8,128)(2,1)}), bf16[16,384,128]{2,1,0:T(8,128)(2,1)S(1)}, u32[]{:S(2)}, u32[]{:S(2)}) async-start(bf16[16,384,128]{2,1,0:T(8,128)(2,1)} %attend_backward.1.order_ref.refs_4_), calls=%async_computation.4 | async-start | bytes 3145728 | tf_op jit(solution)/shard_map/all_to_all | solution.py:488
  139.1 15.6 %collective-permute-start.10 = (bf16[128,768]{1,0:T(8,128)(2,1)S(1)}, bf16[128,768]{1,0:T(8,128)(2,1)S(1)}, u32[]{:S(2)}, u32[]{:S(2)}) collective-permute-start(bf16[128,768]{1,0:T(8,128)(2,1)S(1)} %copy-done.7), channel_id=1, source_target_pairs={{0,128},{128,0},{1,129},{129,1},{2,130},{130,2},{3,131},{131,3},{4... | collective-permute-start | bytes 589832 | tf_op jit(solution)/shard_map/ppermute | solution.py:421
  150.5 6.7 %collective-permute-start.15 = (bf16[128,768]{1,0:T(8,128)(2,1)}, bf16[128,768]{1,0:T(8,128)(2,1)S(1)}, u32[]{:S(2)}, u32[]{:S(2)}) collective-permute-start(bf16[128,768]{1,0:T(8,128)(2,1)} %get-tuple-element.42), channel_id=1, source_target_pairs={{0,8},{1,9},{2,10},{3,11},{4,12},{5,13},{6,14},{7,15},{8,64},{9,65... | collective-permute-start | bytes 589832 | tf_op jit(solution)/shard_map/ppermute | solution.py:436
  151.5 16.6 %collective-permute-start.16 = (bf16[128,768]{1,0:T(8,128)(2,1)}, bf16[128,768]{1,0:T(8,128)(2,1)S(1)}, u32[]{:S(2)}, u32[]{:S(2)}) collective-permute-start(bf16[128,768]{1,0:T(8,128)(2,1)} %get-tuple-element.43), channel_id=1, source_target_pairs={{0,64},{1,65},{2,66},{3,67},{4,68},{5,69},{6,70},{7,71},{8,72},{9,... | collective-permute-start | bytes 589832 | tf_op jit(solution)/shard_map/ppermute | solution.py:436
  153.7 15.4 %collective-permute-start.17 = (bf16[128,768]{1,0:T(8,128)(2,1)}, bf16[128,768]{1,0:T(8,128)(2,1)S(1)}, u32[]{:S(2)}, u32[]{:S(2)}) collective-permute-start(bf16[128,768]{1,0:T(8,128)(2,1)} %get-tuple-element.44), channel_id=1, source_target_pairs={{0,72},{1,73},{2,74},{3,75},{4,76},{5,77},{6,78},{7,79},{8,0},{9,1... | collective-permute-start | bytes 589832 | tf_op jit(solution)/shard_map/ppermute | solution.py:436
  171.8 8.6 %collective-permute-start.18 = (bf16[64,768]{1,0:T(8,128)(2,1)}, bf16[64,768]{1,0:T(8,128)(2,1)S(1)}, u32[]{:S(2)}, u32[]{:S(2)}) collective-permute-start(bf16[64,768]{1,0:T(8,128)(2,1)} %get-tuple-element.46), channel_id=1, source_target_pairs={{0,4},{1,5},{2,6},{3,7},{4,0},{5,1},{6,2},{7,3},{8,12},{9,13},{10,... | collective-permute-start | bytes 294920 | tf_op jit(solution)/shard_map/ppermute | solution.py:479
  188.1 6.6 %collective-permute-start.22 = (f32[16,768]{1,0:T(8,128)S(1)}, f32[16,768]{1,0:T(8,128)S(1)}, u32[]{:S(2)}, u32[]{:S(2)}) collective-permute-start(f32[16,768]{1,0:T(8,128)S(1)} %total_of.1.own_ref), channel_id=1, source_target_pairs={{0,128},{128,0},{1,129},{129,1},{2,130},{130,2},{3,131},{131,3},{4... | collective-permute-start | bytes 147464 | tf_op jit(solution)/shard_map/ppermute | solution.py:421
  (18 other events, 147.1 us)
where the time goes:
time: 197 us; the launch traced here: 196 us
  waiting for transfers between devices  76.2 us (39%)
  starting transfers between devices  67.7 us (34%)
  Pallas kernels  44.9 us (23%)
  local copies, waits for them, and re-layouts  3.86 us (2%)
  between operations  2.22 us (1%)
    ppermute x6, waiting for transfers between devices, shift_x(): return lax.ppermute(value, ('fsdp', 'seq'), pairs)  23 us
    all_to_all x4, starting transfers between devices, over_seq(): return lax.all_to_all(array, 'seq', split_axis=0, concat_axis=0, tiled=True)  21.9 us
    all_to_all x4, waiting for transfers between devices, over_seq(): return lax.all_to_all(array, 'seq', split_axis=0, concat_axis=0, tiled=True)  21.1 us
    ppermute x9, waiting for transfers between devices, shift_y(): return lax.ppermute(value, 'fsdp', pairs)  14.6 us
    ppermute x9, starting transfers between devices, shift_y(): return lax.ppermute(value, 'fsdp', pairs)  13.9 us
    pallas_call x1, Pallas kernels, attend_backward(): call(backward_kernel, 'attend_backward', kept(qkv.shape), [full(qkv), ful...  12.9 us
    pallas_call x1, Pallas kernels, attend_forward(): call(forward_kernel, 'attend_forward', (kept((shards, rows, HDIM)), spill...  9.61 us
    ppermute x4, starting transfers between devices, swap_cfg(): return lax.ppermute(value, 'cfg', [(0, 1), (1, 0)])  9.51 us
  transfers between devices with their start and end apart: 28, of which 14 were waited for; matrix products, arithmetic and copies ran while one was open for 0% of the time, Pallas kernels for 15%

commit v1 on v0

--- a/solution.py
+++ b/solution.py
@@ -132,10 +132,15 @@
     scale = HDIM ** (-0.5) * LOG2E
     take = CHUNK // rows
     copies = []
-    for part in range(length // CHUNK):
-        here = slice(part * take, (part + 1) * take)
-        query = qkv_ref[here, :rows, :].reshape(CHUNK, HDIM)
-        scores = lax.dot_general(keys, query, NT, preferred_element_type=F32)
+
+    def scores_of(part):
+        query = qkv_ref[part * take : (part + 1) * take, :rows, :].reshape(CHUNK, HDIM)
+        return lax.dot_general(keys, query, NT, preferred_element_type=F32)
+
+    parts = length // CHUNK
+    scores = scores_of(0)
+    for part in range(parts):
+        later = scores_of(part + 1) if part + 1 < parts else None
         peak = jnp.max(scores, axis=0, keepdims=True) * scale
         weights = jnp.exp2(scores * scale - peak)
         total = jnp.sum(weights, axis=0, keepdims=True)
@@ -146,7 +151,8 @@
         copy.start()
         copies.append(copy)
         mixed_t = jnp.dot(value_t, probs, preferred_element_type=F32)
-        out_ref[here] = mixed_t.T.astype(BF).reshape(take, rows, HDIM)
+        out_ref[part * take : (part + 1) * take] = mixed_t.T.astype(BF).reshape(take, rows, HDIM)
+        scores = later
     for copy in copies:
         copy.wait()
 
@@ -354,52 +360,48 @@
     return call(add_kernel, "add_after", kept(got.shape), whole(2))(pin(keep), pin(got))
 
 
-def halves_kernel(place_ref, *refs):
-    arrays, keep_ref, send_ref, held = refs[:4], refs[-3], refs[-2], refs[-1]
-    rows = keep_ref.shape[0]
+def quads_kernel(place_ref, *refs):
+    arrays, out_refs, held = refs[:4], refs[5:-1], refs[-1]
+    deep = out_refs[0].shape[1]
     held[...] = sum(ref[...].astype(F32) for ref in arrays)
-    start = pl.multiple_of((place_ref[17] >> 2) * rows, rows)
-    other = pl.multiple_of(rows - start, rows)
-    keep_ref[...] = held[pl.ds(start, rows), :]
-    send_ref[...] = held[pl.ds(other, rows), :].astype(BF)
-
-
-def z_halves(place, arrays, order):
+    for step, ref in enumerate(out_refs):
+        low = (place_ref[17] + step) & 3
+        for high in range(2):
+            start = pl.multiple_of((4 * high + low) * deep, deep)
+            ref[high] = held[pl.ds(start, deep), :].astype(ref.dtype)
+
+
+def z_quads(place, arrays, order):
     rows, wide = arrays[0].shape
-    outs = (spilled((rows // 2, wide), F32), spilled((rows // 2, wide)))
-    return call(
-        halves_kernel,
-        "z_halves",
-        outs,
+    target = (2, rows // 8, wide)
+    return call(
+        quads_kernel,
+        "z_quads",
+        (kept(target, F32),) + (kept(target),) * 3,
         [scalars_spec()] + [full(array) for array in arrays] + [anywhere()],
-        [full(target) for target in outs],
+        whole(4),
         grid=(1,),
         flops=10000000000,
         scratch_shapes=[pltpu.VMEM((rows, wide), F32)],
     )(place, *[out(array) for array in arrays], out(order))
 
 
-def quarters_kernel(place_ref, keep_ref, got_ref, *refs):
-    out_refs, held = refs[:-1], refs[-1]
-    deep = out_refs[0].shape[0]
-    held[...] = keep_ref[...] + got_ref[...].astype(F32)
-    for step, ref in enumerate(out_refs):
-        start = pl.multiple_of(((place_ref[17] + step) & 3) * deep, deep)
-        ref[...] = held[pl.ds(start, deep), :].astype(ref.dtype)
-
-
-def z_quarters(place, keep, got):
-    rows, wide = keep.shape
-    target = (rows // 4, wide)
-    return call(
-        quarters_kernel,
-        "z_quarters",
-        (kept(target, F32),) + (kept(target),) * 3,
-        [scalars_spec(), full(keep), full(got)],
-        whole(4),
-        grid=(1,),
-        scratch_shapes=[pltpu.VMEM((rows, wide), F32)],
-    )(place, keep, got)
+def pair_kernel(place_ref, *refs):
+    in_refs, keep_ref, send_ref = refs[:4], refs[4], refs[5]
+    total = sum(ref[...].astype(F32) for ref in in_refs)
+    first = (place_ref[17] >> 2) == 0
+    keep_ref[...] = jnp.where(first, total[0], total[1])
+    send_ref[...] = jnp.where(first, total[1], total[0]).astype(BF)
+
+
+def z_pair(place, parts):
+    shape = parts[0].shape[1:]
+    return call(
+        pair_kernel,
+        "z_pair",
+        (kept(shape, F32), kept(shape)),
+        [scalars_spec()] + whole(4),
+    )(place, *[pin(part) for part in parts])
 
 
 def total_kernel(*refs):
@@ -415,6 +417,26 @@
         whole(len(arrays)),
         whole(1)[0],
     )(*[pin(array) for array in arrays])
+
+
+def spread_kernel(weight_ref, out_ref):
+    half = out_ref.shape[2]
+    first = lax.axis_index("cfg") == 0
+    own = jnp.where(first, weight_ref[:, :half], weight_ref[:, half:])
+    for target in range(out_ref.shape[0]):
+        out_ref[target] = own
+
+
+def spread(weight):
+    rows, width = weight.shape
+    return call(
+        spread_kernel,
+        "spread",
+        spilled((8, rows, width // 2)),
+        [full(weight)],
+        pl.BlockSpec((8, rows, width // 2), lambda i: (0, 0, 0)),
+        grid=(1,),
+    )(out(weight))
 
 
 def swap_cfg(value):
@@ -475,13 +497,12 @@
 def scatter_rest(place, groups, order, packed):
     sums = group_sums(groups, packed)
     ring = [sums[0]] + [shift_x(sums[step], step) for step in range(1, 4)]
-    keep, send = z_halves(place, ring, order)
-    got = lax.ppermute(send, "seq", [(i, i ^ 4) for i in range(16)])
-    parts = list(z_quarters(place, keep, got))
+    parts = list(z_quads(place, ring, order))
     for step in range(1, 4):
         pairs = [(i, (i & 12) + ((i + step) & 3)) for i in range(16)]
         parts[step] = lax.ppermute(parts[step], "seq", pairs)
-    return total_of(parts)
+    keep, send = z_pair(place, parts)
+    return total_of([keep, lax.ppermute(send, "seq", [(i, i ^ 4) for i in range(16)])])
 
 
 def over_seq(array):
@@ -533,8 +554,7 @@
     strength = 1.0 + GUIDE_STEP * guide_index[0].astype(F32)
     scalars = jnp.stack([gate, strength])
     half = out_weight.shape[1] // 2
-    own_half = jnp.where(place[0] == 0, out_weight[:, :half], out_weight[:, half:])
-    piece = over_z(jnp.broadcast_to(own_half[None], (8,) + own_half.shape)).reshape(-1, half)
+    piece = over_z(spread(out_weight)).reshape(-1, half)
     groups = gather_groups(piece)
     qkv = over_seq(pack_heads(query_act[0, 0], key_act[0, 0], value_act[0, 0]))
     mixed_h, probs = attend_forward(qkv, groups[1], groups[3], groups[5], groups[7], place, scalars)

time: 197 us -> 194 us (0.985)
  waiting for transfers between devices: 76.2 us -> 70.7 us
  starting transfers between devices: 67.7 us -> 72.2 us
    ppermute x1, waiting for transfers between devices: 8.62 us -> 2.46 us  [scatter_rest(): lax.ppermute(send, 'seq', [(i, i ^ 4) for i in range(16)])]
    ppermute x1, starting transfers between devices: 0.01 us -> 4.44 us  [scatter_rest(): lax.ppermute(send, 'seq', [(i, i ^ 4) for i in range(16)])]
  transfers between devices with their start and end apart: 28 -> 28, of which waited for: 14 -> 16; matrix products, arithmetic and copies ran while one was open for 0% -> 0% of each run, Pallas kernels for 15% -> 15%
where the time goes in v1:
time: 194 us; the launch traced here: 193 us
  starting transfers between devices  72.2 us (37%)
  waiting for transfers between devices  70.7 us (36%)
  Pallas kernels  45.3 us (23%)
  local copies, waits for them, and re-layouts  2.26 us (1%)
  between operations  2.22 us (1%)
    ppermute x6, waiting for transfers between devices, shift_x(): return lax.ppermute(value, ('fsdp', 'seq'), pairs)  23 us
    all_to_all x4, starting transfers between devices, over_seq(): return lax.all_to_all(array, 'seq', split_axis=0, concat_axis=0, tiled=True)  21.9 us
    all_to_all x4, waiting for transfers between devices, over_seq(): return lax.all_to_all(array, 'seq', split_axis=0, concat_axis=0, tiled=True)  21.1 us
    ppermute x9, waiting for transfers between devices, shift_y(): return lax.ppermute(value, 'fsdp', pairs)  14.7 us
    ppermute x9, starting transfers between devices, shift_y(): return lax.ppermute(value, 'fsdp', pairs)  13.9 us
    pallas_call x1, Pallas kernels, attend_backward(): call(backward_kernel, 'attend_backward', kept(qkv.shape), [full(qkv), ful...  12.9 us
    ppermute x4, starting transfers between devices, swap_cfg(): return lax.ppermute(value, 'cfg', [(0, 1), (1, 0)])  9.51 us
    pallas_call x1, Pallas kernels, attend_forward(): call(forward_kernel, 'attend_forward', (kept((shards, rows, HDIM)), spill...  9.23 us
  transfers between devices with their start and end apart: 28, of which 16 were waited for; matrix products, arithmetic and copies ran while one was open for 0% of the time, Pallas kernels for 15%

profile of v1, /device:TPU:1, one launch (start us, length us, event | category | flops | bytes accessed | tf_op | source)
XLA Modules:
  0.0 193.0 jit_solution(1228288513176689410)
XLA Ops:
  2.1 9.0 %all-to-all-start.1 = ((bf16[8,16,768]{2,1,0:T(8,128)(2,1)}), bf16[8,16,768]{2,1,0:T(8,128)(2,1)S(1)}, u32[]{:S(2)}, u32[]{:S(2)}) async-start(bf16[8,16,768]{2,1,0:T(8,128)(2,1)} %spread.1), calls=%async_computation.1 | async-start | bytes 393216 | tf_op jit(solution)/shard_map/all_to_all | solution.py:514
  11.1 2.8 %pack_heads.1 = bf16[16,384,128]{2,1,0:T(8,128)(2,1)} custom-call(bf16[128,2048]{1,0:T(8,128)(2,1)} %bitcast.20, bf16[128,2048]{1,0:T(8,128)(2,1)} %bitcast.21, bf16[128,2048]{1,0:T(8,128)(2,1)} %bitcast.22), custom_call_target="tpu_custom_call" | custom-call | flops 1 | bytes 1 | tf_op jit(solution)/shard_map/pack_heads/pallas_call | solution.py:94
  13.9 6.0 %all-to-all-done.1 = bf16[8,16,768]{2,1,0:T(8,128)(2,1)S(1)} async-done(((bf16[8,16,768]{2,1,0:T(8,128)(2,1)}), bf16[8,16,768]{2,1,0:T(8,128)(2,1)S(1)}, u32[]{:S(2)}, u32[]{:S(2)}) %all-to-all-start.1) | async-done | bytes 196640 | tf_op jit(solution)/shard_map/all_to_all | solution.py:514
  20.0 4.1 %all-to-all-start = ((bf16[16,384,128]{2,1,0:T(8,128)(2,1)}), bf16[16,384,128]{2,1,0:T(8,128)(2,1)S(1)}, u32[]{:S(2)}, u32[]{:S(2)}) async-start(bf16[16,384,128]{2,1,0:T(8,128)(2,1)} %pack_heads.1), calls=%async_computation | async-start | bytes 3145728 | tf_op jit(solution)/shard_map/all_to_all | solution.py:509
  24.1 2.6 %collective-permute-start = (bf16[128,768]{1,0:T(8,128)(2,1)S(1)}, bf16[128,768]{1,0:T(8,128)(2,1)S(1)}, u32[]{:S(2)}, u32[]{:S(2)}) collective-permute-start(bf16[128,768]{1,0:T(8,128)(2,1)S(1)} %bitcast.15), channel_id=1, source_target_pairs={{0,72},{1,73},{2,74},{3,75},{4,76},{5,77},{6,78},{7,79},{8,0},{9,1... | collective-permute-start | bytes 589832 | tf_op jit(solution)/shard_map/ppermute | solution.py:458
  28.1 7.2 %collective-permute-done = bf16[128,768]{1,0:T(8,128)(2,1)S(1)} collective-permute-done((bf16[128,768]{1,0:T(8,128)(2,1)S(1)}, bf16[128,768]{1,0:T(8,128)(2,1)S(1)}, u32[]{:S(2)}, u32[]{:S(2)}) %collective-permute-start) | collective-permute-done | bytes 196640 | tf_op jit(solution)/shard_map/ppermute | solution.py:458
  38.2 4.0 %collective-permute-done.3 = bf16[128,768]{1,0:T(8,128)(2,1)S(1)} collective-permute-done((bf16[128,768]{1,0:T(8,128)(2,1)S(1)}, bf16[128,768]{1,0:T(8,128)(2,1)S(1)}, u32[]{:S(2)}, u32[]{:S(2)}) %collective-permute-start.3) | collective-permute-done | bytes 196640 | tf_op jit(solution)/shard_map/ppermute | solution.py:458
  46.9 7.8 %collective-permute-done.6.refs_3_.refs_7_ = bf16[2,128,768]{2,1,0:T(8,128)(2,1)S(1)} collective-permute-done((bf16[2,128,768]{2,1,0:T(8,128)(2,1)S(1)}, bf16[2,128,768]{2,1,0:T(8,128)(2,1)S(1)}, u32[]{:S(2)}, u32[]{:S(2)}) %collective-permute-start.6) | collective-permute-done | bytes 393248 | tf_op jit(solution)/shard_map/ppermute | solution.py:448
  54.8 5.4 %all-to-all-done.qkv_ref = bf16[16,384,128]{2,1,0:T(8,128)(2,1)S(1)} async-done(((bf16[16,384,128]{2,1,0:T(8,128)(2,1)}), bf16[16,384,128]{2,1,0:T(8,128)(2,1)S(1)}, u32[]{:S(2)}, u32[]{:S(2)}) %all-to-all-start) | async-done | bytes 1572896 | tf_op jit(solution)/shard_map/all_to_all | solution.py:509
  60.1 9.2 %attend_forward.1 = (bf16[16,128,128]{2,1,0:T(8,128)(2,1)}, bf16[2048,2048]{1,0:T(8,128)(2,1)}) custom-call(bf16[16,384,128]{2,1,0:T(8,128)(2,1)S(1)} %all-to-all-done.qkv_ref, bf16[2,128,768]{2,1,0:T(8,128)(2,1)} %copy-done.4, bf16[2,128,768]{2,1,0:T(8,128)(2,1)} %copy-done.3, bf16[2,128,768]{2,1,0:T(8,128)(2,1)} %collective-permute-done.5.refs_2_.refs_5_, ...), custom_call_target="tpu_custom_call" | custom-call | flops 1 | bytes 1 | tf_op jit(solution)/shard_map/attend_forward/pallas_call | solution.py:164
  69.4 6.4 %all-to-all-start.2 = ((bf16[16,128,128]{2,1,0:T(8,128)(2,1)}), bf16[16,128,128]{2,1,0:T(8,128)(2,1)S(1)}, u32[]{:S(2)}, u32[]{:S(2)}) async-start(bf16[16,128,128]{2,1,0:T(8,128)(2,1)} %get-tuple-element.28.mixed_ref), calls=%async_computation.2 | async-start | bytes 1048576 | tf_op jit(solution)/shard_map/all_to_all | solution.py:509
  78.7 9.9 %all-to-all-done.2.refs_8_.own_ref = bf16[16,128,128]{2,1,0:T(8,128)(2,1)S(1)} async-done(((bf16[16,128,128]{2,1,0:T(8,128)(2,1)}), bf16[16,128,128]{2,1,0:T(8,128)(2,1)S(1)}, u32[]{:S(2)}, u32[]{:S(2)}) %all-to-all-start.2) | async-done | bytes 524320 | tf_op jit(solution)/shard_map/all_to_all | solution.py:509
  88.6 3.6 %collective-permute-start.7 = (bf16[16,128,128]{2,1,0:T(8,128)(2,1)S(1)}, bf16[16,128,128]{2,1,0:T(8,128)(2,1)S(1)}, u32[]{:S(2)}, u32[]{:S(2)}) collective-permute-start(bf16[16,128,128]{2,1,0:T(8,128)(2,1)S(1)} %all-to-all-done.2.refs_8_.own_ref), channel_id=1, source_target_pairs={{0,128},{128,0},{1,129},{129,1},{2,130},{130,2},{3,131},{131,3},{4... | collective-permute-start | bytes 1572872 | tf_op jit(solution)/shard_map/ppermute | solution.py:443
  94.0 3.8 %project.1 = (bf16[128,768]{1,0:T(8,128)(2,1)}, bf16[256,768]{1,0:T(8,128)(2,1)S(1)}, f32[16,128,128]{2,1,0:T(8,128)S(1)}, bf16[16,128,128]{2,1,0:T(8,128)(2,1)S(1)}) custom-call(s32[18]{0:T(128)S(1)} %pad_add_fusion.refs_4_.place_ref, f32[2]{0:T(128)S(1)} %pad_maximum_fusion.2.refs_5_.scalar_ref, bf16[16,128,128]{2,1,0:T(8,128)(2,1)S(1)} %all-to-all-done.2.refs_8_.own_ref, ...), custom_call_target="tpu_custom_call" | custom-call | flops 1 | bytes 1 | tf_op jit(solution)/shard_map/project/pallas_call | solution.py:319
  100.6 4.6 %all-to-all-start.3 = ((bf16[16,128,128]{2,1,0:T(8,128)(2,1)}), bf16[16,128,128]{2,1,0:T(8,128)(2,1)S(1)}, u32[]{:S(2)}, u32[]{:S(2)}) async-start(bf16[16,128,128]{2,1,0:T(8,128)(2,1)} %add_after.1.order_ref), calls=%async_computation.3 | async-start | bytes 1048576 | tf_op jit(solution)/shard_map/all_to_all | solution.py:509
  105.2 2.9 %weight_gradient.1 = (bf16[4,128,768]{2,1,0:T(8,128)(2,1)}, bf16[4,128,768]{2,1,0:T(8,128)(2,1)}, bf16[4,128,768]{2,1,0:T(8,128)(2,1)}, bf16[4,128,768]{2,1,0:T(8,128)(2,1)}) custom-call(s32[18]{0:T(128)S(1)} %pad_add_fusion.refs_4_.place_ref, bf16[16,128,128]{2,1,0:T(8,128)(2,1)S(1)} %all-to-all-done.2.refs_8_.own_ref, ...), custom_call_target="tpu_custom_call" | custom-call | flops 1 | bytes 1 | tf_op jit(solution)/shard_map/weight_gradient/pallas_call | solution.py:345
  113.1 5.9 %all-to-all-done.3.grad_ref = bf16[16,128,128]{2,1,0:T(8,128)(2,1)S(1)} async-done(((bf16[16,128,128]{2,1,0:T(8,128)(2,1)}), bf16[16,128,128]{2,1,0:T(8,128)(2,1)S(1)}, u32[]{:S(2)}, u32[]{:S(2)}) %all-to-all-start.3) | async-done | bytes 524320 | tf_op jit(solution)/shard_map/all_to_all | solution.py:509
  119.0 12.9 %attend_backward.1.order_ref.refs_4_ = bf16[16,384,128]{2,1,0:T(8,128)(2,1)} custom-call(bf16[16,384,128]{2,1,0:T(8,128)(2,1)} %copy-done, bf16[16,128,128]{2,1,0:T(8,128)(2,1)} %get-tuple-element.28.mixed_ref, bf16[16,128,128]{2,1,0:T(8,128)(2,1)S(1)} %all-to-all-done.3.grad_ref, bf16[2048,2048]{1,0:T(8,128)(2,1)} %get-tuple-element.32.probs_ref, ...), custom_call_target="tpu_custom_call" | custom-call | flops 8589934592 | bytes 1 | tf_op jit(solution)/shard_map/attend_backward/pallas_call | solution.py:222
  131.9 6.8 %all-to-all-start.4 = ((bf16[16,384,128]{2,1,0:T(8,128)(2,1)}), bf16[16,384,128]{2,1,0:T(8,128)(2,1)S(1)}, u32[]{:S(2)}, u32[]{:S(2)}) async-start(bf16[16,384,128]{2,1,0:T(8,128)(2,1)} %attend_backward.1.order_ref.refs_4_), calls=%async_computation.4 | async-start | bytes 3145728 | tf_op jit(solution)/shard_map/all_to_all | solution.py:509
  139.6 6.7 %collective-permute-done.13.refs_2_ = bf16[4,128,768]{2,1,0:T(8,128)(2,1)S(1)} collective-permute-done((bf16[4,128,768]{2,1,0:T(8,128)(2,1)}, bf16[4,128,768]{2,1,0:T(8,128)(2,1)S(1)}, u32[]{:S(2)}, u32[]{:S(2)}) %collective-permute-start.13) | collective-permute-done | bytes 786464 | tf_op jit(solution)/shard_map/ppermute | solution.py:448
  147.2 2.9 %group_sums.1 = (f32[128,768]{1,0:T(8,128)}, bf16[128,768]{1,0:T(8,128)(2,1)}, bf16[128,768]{1,0:T(8,128)(2,1)}, bf16[128,768]{1,0:T(8,128)(2,1)}) custom-call(bf16[4,128,768]{2,1,0:T(8,128)(2,1)} %get-tuple-element.34.refs_0_, bf16[4,128,768]{2,1,0:T(8,128)(2,1)} %copy-done.8, bf16[4,128,768]{2,1,0:T(8,128)(2,1)} %copy-done.9, ...), custom_call_target="tpu_custom_call" | custom-call | flops 10000000000 | bytes 1 | tf_op jit(solution)/shard_map/group_sums/pallas_call | solution.py:482
  156.8 11.1 %collective-permute-done.16.refs_2_ = bf16[128,768]{1,0:T(8,128)(2,1)S(1)} collective-permute-done((bf16[128,768]{1,0:T(8,128)(2,1)}, bf16[128,768]{1,0:T(8,128)(2,1)S(1)}, u32[]{:S(2)}, u32[]{:S(2)}) %collective-permute-start.16) | collective-permute-done | bytes 196640 | tf_op jit(solution)/shard_map/ppermute | solution.py:458
  178.3 4.4 %collective-permute-start.21 = (bf16[16,768]{1,0:T(8,128)(2,1)S(1)}, bf16[16,768]{1,0:T(8,128)(2,1)S(1)}, u32[]{:S(2)}, u32[]{:S(2)}) collective-permute-start(bf16[16,768]{1,0:T(8,128)(2,1)S(1)} %get-tuple-element.50), channel_id=1, source_target_pairs={{0,4},{1,5},{2,6},{3,7},{4,0},{5,1},{6,2},{7,3},{8,12},{9,13},{10,... | collective-permute-start | bytes 73736 | tf_op jit(solution)/shard_map/ppermute | solution.py:505
  185.2 5.0 %collective-permute-start.22 = (f32[16,768]{1,0:T(8,128)S(1)}, f32[16,768]{1,0:T(8,128)S(1)}, u32[]{:S(2)}, u32[]{:S(2)}) collective-permute-start(f32[16,768]{1,0:T(8,128)S(1)} %total_of.1.own_ref), channel_id=1, source_target_pairs={{0,128},{128,0},{1,129},{129,1},{2,130},{130,2},{3,131},{131,3},{4... | collective-permute-start | bytes 147464 | tf_op jit(solution)/shard_map/ppermute | solution.py:443
  (78 shorter events, 45.7 us)
Async XLA Ops:
  2.1 17.8 %all-to-all-start.1 = ((bf16[8,16,768]{2,1,0:T(8,128)(2,1)}), bf16[8,16,768]{2,1,0:T(8,128)(2,1)S(1)}, u32[]{:S(2)}, u32[]{:S(2)}) async-start(bf16[8,16,768]{2,1,0:T(8,128)(2,1)} %spread.1), calls=%async_computation.1 | async-start | bytes 393216 | tf_op jit(solution)/shard_map/all_to_all | solution.py:514
  20.0 40.2 %all-to-all-start = ((bf16[16,384,128]{2,1,0:T(8,128)(2,1)}), bf16[16,384,128]{2,1,0:T(8,128)(2,1)S(1)}, u32[]{:S(2)}, u32[]{:S(2)}) async-start(bf16[16,384,128]{2,1,0:T(8,128)(2,1)} %pack_heads.1), calls=%async_computation | async-start | bytes 3145728 | tf_op jit(solution)/shard_map/all_to_all | solution.py:509
  24.1 11.2 %collective-permute-start = (bf16[128,768]{1,0:T(8,128)(2,1)S(1)}, bf16[128,768]{1,0:T(8,128)(2,1)S(1)}, u32[]{:S(2)}, u32[]{:S(2)}) collective-permute-start(bf16[128,768]{1,0:T(8,128)(2,1)S(1)} %bitcast.15), channel_id=1, source_target_pairs={{0,72},{1,73},{2,74},{3,75},{4,76},{5,77},{6,78},{7,79},{8,0},{9,1... | collective-permute-start | bytes 589832 | tf_op jit(solution)/shard_map/ppermute | solution.py:458
  26.7 11.5 %collective-permute-start.4 = (bf16[128,768]{1,0:T(8,128)(2,1)S(1)}, bf16[128,768]{1,0:T(8,128)(2,1)S(1)}, u32[]{:S(2)}, u32[]{:S(2)}) collective-permute-start(bf16[128,768]{1,0:T(8,128)(2,1)S(1)} %bitcast.16), channel_id=1, source_target_pairs={{0,8},{1,9},{2,10},{3,11},{4,12},{5,13},{6,14},{7,15},{8,64},{9,65... | collective-permute-start | bytes 589832 | tf_op jit(solution)/shard_map/ppermute | solution.py:458
  26.7 15.5 %collective-permute-start.3 = (bf16[128,768]{1,0:T(8,128)(2,1)S(1)}, bf16[128,768]{1,0:T(8,128)(2,1)S(1)}, u32[]{:S(2)}, u32[]{:S(2)}) collective-permute-start(bf16[128,768]{1,0:T(8,128)(2,1)S(1)} %bitcast.17), channel_id=1, source_target_pairs={{0,64},{1,65},{2,66},{3,67},{4,68},{5,69},{6,70},{7,71},{8,72},{9,... | collective-permute-start | bytes 589832 | tf_op jit(solution)/shard_map/ppermute | solution.py:458
  35.3 11.6 %collective-permute-start.2 = (bf16[2,128,768]{2,1,0:T(8,128)(2,1)S(1)}, bf16[2,128,768]{2,1,0:T(8,128)(2,1)S(1)}, u32[]{:S(2)}, u32[]{:S(2)}) collective-permute-start(bf16[2,128,768]{2,1,0:T(8,128)(2,1)S(1)} %pad_maximum_fusion.refs_0_), channel_id=1, source_target_pairs={{0,16},{16,32},{32,48},{48,0},{64,80},{80,96},{96,112},{112,64},{1... | collective-permute-start | bytes 1179656 | tf_op jit(solution)/shard_map/ppermute | solution.py:448
  36.7 10.2 %collective-permute-start.1 = (bf16[2,128,768]{2,1,0:T(8,128)(2,1)S(1)}, bf16[2,128,768]{2,1,0:T(8,128)(2,1)S(1)}, u32[]{:S(2)}, u32[]{:S(2)}) collective-permute-start(bf16[2,128,768]{2,1,0:T(8,128)(2,1)S(1)} %pad_maximum_fusion.refs_0_), channel_id=1, source_target_pairs={{0,48},{16,0},{32,16},{48,32},{64,112},{80,64},{96,80},{112,96},{1... | collective-permute-start | bytes 1179656 | tf_op jit(solution)/shard_map/ppermute | solution.py:448
  42.2 12.5 %collective-permute-start.6 = (bf16[2,128,768]{2,1,0:T(8,128)(2,1)S(1)}, bf16[2,128,768]{2,1,0:T(8,128)(2,1)S(1)}, u32[]{:S(2)}, u32[]{:S(2)}) collective-permute-start(bf16[2,128,768]{2,1,0:T(8,128)(2,1)S(1)} %pad_maximum_fusion.1.refs_4_), channel_id=1, source_target_pairs={{0,16},{16,32},{32,48},{48,0},{64,80},{80,96},{96,112},{112,64},{1... | collective-permute-start | bytes 1179656 | tf_op jit(solution)/shard_map/ppermute | solution.py:448
  43.6 11.2 %collective-permute-start.5 = (bf16[2,128,768]{2,1,0:T(8,128)(2,1)S(1)}, bf16[2,128,768]{2,1,0:T(8,128)(2,1)}, u32[]{:S(2)}, u32[]{:S(2)}) collective-permute-start(bf16[2,128,768]{2,1,0:T(8,128)(2,1)S(1)} %pad_maximum_fusion.1.refs_4_), channel_id=1, source_target_pairs={{0,48},{16,0},{32,16},{48,32},{64,112},{80,64},{96,80},{112,96},{1... | collective-permute-start | bytes 1179656 | tf_op jit(solution)/shard_map/ppermute | solution.py:448
  69.4 19.2 %all-to-all-start.2 = ((bf16[16,128,128]{2,1,0:T(8,128)(2,1)}), bf16[16,128,128]{2,1,0:T(8,128)(2,1)S(1)}, u32[]{:S(2)}, u32[]{:S(2)}) async-start(bf16[16,128,128]{2,1,0:T(8,128)(2,1)} %get-tuple-element.28.mixed_ref), calls=%async_computation.2 | async-start | bytes 1048576 | tf_op jit(solution)/shard_map/all_to_all | solution.py:509
  75.8 16.3 %collective-permute-start.8 = (bf16[2,128,768]{2,1,0:T(8,128)(2,1)}, bf16[2,128,768]{2,1,0:T(8,128)(2,1)S(1)}, u32[]{:S(2)}, u32[]{:S(2)}) collective-permute-start(bf16[2,128,768]{2,1,0:T(8,128)(2,1)} %copy-done.3), channel_id=1, source_target_pairs={{0,16},{16,32},{32,48},{48,0},{64,80},{80,96},{96,112},{112,64},{1... | collective-permute-start | bytes 1179656 | tf_op jit(solution)/shard_map/ppermute | solution.py:448
  77.2 15.0 %collective-permute-start.9 = (bf16[2,128,768]{2,1,0:T(8,128)(2,1)}, bf16[2,128,768]{2,1,0:T(8,128)(2,1)S(1)}, u32[]{:S(2)}, u32[]{:S(2)}) collective-permute-start(bf16[2,128,768]{2,1,0:T(8,128)(2,1)} %collective-permute-done.5.refs_2_.refs_5_), channel_id=1, source_target_pairs={{0,48},{16,0},{32,16},{48,32},{64,112},{80,64},{96,80},{112,96},{1... | collective-permute-start | bytes 1179656 | tf_op jit(solution)/shard_map/ppermute | solution.py:448
  100.6 18.4 %all-to-all-start.3 = ((bf16[16,128,128]{2,1,0:T(8,128)(2,1)}), bf16[16,128,128]{2,1,0:T(8,128)(2,1)S(1)}, u32[]{:S(2)}, u32[]{:S(2)}) async-start(bf16[16,128,128]{2,1,0:T(8,128)(2,1)} %add_after.1.order_ref), calls=%async_computation.3 | async-start | bytes 1048576 | tf_op jit(solution)/shard_map/all_to_all | solution.py:509
  108.1 31.4 %collective-permute-start.12 = (bf16[4,128,768]{2,1,0:T(8,128)(2,1)}, bf16[4,128,768]{2,1,0:T(8,128)(2,1)S(1)}, u32[]{:S(2)}, u32[]{:S(2)}) collective-permute-start(bf16[4,128,768]{2,1,0:T(8,128)(2,1)} %get-tuple-element.38), channel_id=1, source_target_pairs={{0,16},{16,32},{32,48},{48,0},{64,80},{80,96},{96,112},{112,64},{1... | collective-permute-start | bytes 2359304 | tf_op jit(solution)/shard_map/ppermute | solution.py:448
  109.4 36.9 %collective-permute-start.13 = (bf16[4,128,768]{2,1,0:T(8,128)(2,1)}, bf16[4,128,768]{2,1,0:T(8,128)(2,1)S(1)}, u32[]{:S(2)}, u32[]{:S(2)}) collective-permute-start(bf16[4,128,768]{2,1,0:T(8,128)(2,1)} %get-tuple-element.39), channel_id=1, source_target_pairs={{0,32},{16,48},{32,0},{48,16},{64,96},{80,112},{96,64},{112,80},{1... | collective-permute-start | bytes 2359304 | tf_op jit(solution)/shard_map/ppermute | solution.py:448
  112.0 34.3 %collective-permute-start.14 = (bf16[4,128,768]{2,1,0:T(8,128)(2,1)}, bf16[4,128,768]{2,1,0:T(8,128)(2,1)}, u32[]{:S(2)}, u32[]{:S(2)}) collective-permute-start(bf16[4,128,768]{2,1,0:T(8,128)(2,1)} %get-tuple-element.40), channel_id=1, source_target_pairs={{0,48},{16,0},{32,16},{48,32},{64,112},{80,64},{96,80},{112,96},{1... | collective-permute-start | bytes 2359304 | tf_op jit(solution)/shard_map/ppermute | solution.py:448
  131.9 58.3 %all-to-all-start.4 = ((bf16[16,384,128]{2,1,0:T(8,128)(2,1)}), bf16[16,384,128]{2,1,0:T(8,128)(2,1)S(1)}, u32[]{:S(2)}, u32[]{:S(2)}) async-start(bf16[16,384,128]{2,1,0:T(8,128)(2,1)} %attend_backward.1.order_ref.refs_4_), calls=%async_computation.4 | async-start | bytes 3145728 | tf_op jit(solution)/shard_map/all_to_all | solution.py:509
  138.7 15.6 %collective-permute-start.10 = (bf16[128,768]{1,0:T(8,128)(2,1)S(1)}, bf16[128,768]{1,0:T(8,128)(2,1)S(1)}, u32[]{:S(2)}, u32[]{:S(2)}) collective-permute-start(bf16[128,768]{1,0:T(8,128)(2,1)S(1)} %copy-done.6), channel_id=1, source_target_pairs={{0,128},{128,0},{1,129},{129,1},{2,130},{130,2},{3,131},{131,3},{4... | collective-permute-start | bytes 589832 | tf_op jit(solution)/shard_map/ppermute | solution.py:443
  150.1 6.7 %collective-permute-start.15 = (bf16[128,768]{1,0:T(8,128)(2,1)}, bf16[128,768]{1,0:T(8,128)(2,1)S(1)}, u32[]{:S(2)}, u32[]{:S(2)}) collective-permute-start(bf16[128,768]{1,0:T(8,128)(2,1)} %get-tuple-element.42), channel_id=1, source_target_pairs={{0,8},{1,9},{2,10},{3,11},{4,12},{5,13},{6,14},{7,15},{8,64},{9,65... | collective-permute-start | bytes 589832 | tf_op jit(solution)/shard_map/ppermute | solution.py:458
  151.1 16.8 %collective-permute-start.16 = (bf16[128,768]{1,0:T(8,128)(2,1)}, bf16[128,768]{1,0:T(8,128)(2,1)S(1)}, u32[]{:S(2)}, u32[]{:S(2)}) collective-permute-start(bf16[128,768]{1,0:T(8,128)(2,1)} %get-tuple-element.43), channel_id=1, source_target_pairs={{0,64},{1,65},{2,66},{3,67},{4,68},{5,69},{6,70},{7,71},{8,72},{9,... | collective-permute-start | bytes 589832 | tf_op jit(solution)/shard_map/ppermute | solution.py:458
  153.3 15.4 %collective-permute-start.17 = (bf16[128,768]{1,0:T(8,128)(2,1)}, bf16[128,768]{1,0:T(8,128)(2,1)S(1)}, u32[]{:S(2)}, u32[]{:S(2)}) collective-permute-start(bf16[128,768]{1,0:T(8,128)(2,1)} %get-tuple-element.44), channel_id=1, source_target_pairs={{0,72},{1,73},{2,74},{3,75},{4,76},{5,77},{6,78},{7,79},{8,0},{9,1... | collective-permute-start | bytes 589832 | tf_op jit(solution)/shard_map/ppermute | solution.py:458
  170.7 6.6 %collective-permute-start.18 = (bf16[2,16,768]{2,1,0:T(8,128)(2,1)S(1)}, bf16[2,16,768]{2,1,0:T(8,128)(2,1)S(1)}, u32[]{:S(2)}, u32[]{:S(2)}) collective-permute-start(bf16[2,16,768]{2,1,0:T(8,128)(2,1)S(1)} %get-tuple-element.46), channel_id=1, source_target_pairs={{0,1},{1,2},{2,3},{3,0},{4,5},{5,6},{6,7},{7,4},{8,9},{9,10},{10,1... | collective-permute-start | bytes 147464 | tf_op jit(solution)/shard_map/ppermute | solution.py:503
  178.3 6.9 %collective-permute-start.21 = (bf16[16,768]{1,0:T(8,128)(2,1)S(1)}, bf16[16,768]{1,0:T(8,128)(2,1)S(1)}, u32[]{:S(2)}, u32[]{:S(2)}) collective-permute-start(bf16[16,768]{1,0:T(8,128)(2,1)S(1)} %get-tuple-element.50), channel_id=1, source_target_pairs={{0,4},{1,5},{2,6},{3,7},{4,0},{5,1},{6,2},{7,3},{8,12},{9,13},{10,... | collective-permute-start | bytes 73736 | tf_op jit(solution)/shard_map/ppermute | solution.py:505
  185.2 6.6 %collective-permute-start.22 = (f32[16,768]{1,0:T(8,128)S(1)}, f32[16,768]{1,0:T(8,128)S(1)}, u32[]{:S(2)}, u32[]{:S(2)}) collective-permute-start(f32[16,768]{1,0:T(8,128)S(1)} %total_of.1.own_ref), channel_id=1, source_target_pairs={{0,128},{128,0},{1,129},{129,1},{2,130},{130,2},{3,131},{131,3},{4... | collective-permute-start | bytes 147464 | tf_op jit(solution)/shard_map/ppermute | solution.py:443
  (17 other events, 146.9 us)

commit v2 on v1

--- a/solution.py
+++ b/solution.py
@@ -128,7 +128,7 @@
     rows = total_rows // 3
     length = shards * rows
     keys = qkv_ref[:, rows : 2 * rows, :].reshape(length, HDIM)
-    value_t = qkv_ref[:, 2 * rows :, :].reshape(length, HDIM).astype(F32).T.astype(BF)
+    value_t = qkv_ref[:, 2 * rows :, :].reshape(length, HDIM).T
     scale = HDIM ** (-0.5) * LOG2E
     take = CHUNK // rows
     copies = []
@@ -151,7 +151,7 @@
         copy.start()
         copies.append(copy)
         mixed_t = jnp.dot(value_t, probs, preferred_element_type=F32)
-        out_ref[part * take : (part + 1) * take] = mixed_t.T.astype(BF).reshape(take, rows, HDIM)
+        out_ref[part * take : (part + 1) * take] = mixed_t.astype(BF).T.reshape(take, rows, HDIM)
         scores = later
     for copy in copies:
         copy.wait()
@@ -213,7 +213,7 @@
         one_chunk(2 * part)
         one_chunk(2 * part + 1)
 
-    grad_query = (query_t[...] * factor).T.astype(BF)
+    grad_query = (query_t[...] * factor).astype(BF).T
     out_ref[:, :rows, :] = grad_query.reshape(shards, rows, HDIM)
 
 

time: 194 us -> 194 us (level)
  no operation moved by 1% of the time
where the time goes in v2:
time: 194 us; the launch traced here: 193 us
  starting transfers between devices  72.2 us (37%)
  waiting for transfers between devices  70.8 us (36%)
  Pallas kernels  45.1 us (23%)
  local copies, waits for them, and re-layouts  2.26 us (1%)
  between operations  2.22 us (1%)
    ppermute x6, waiting for transfers between devices, shift_x(): return lax.ppermute(value, ('fsdp', 'seq'), pairs)  23 us
    all_to_all x4, starting transfers between devices, over_seq(): return lax.all_to_all(array, 'seq', split_axis=0, concat_axis=0, tiled=True)  21.9 us
    all_to_all x4, waiting for transfers between devices, over_seq(): return lax.all_to_all(array, 'seq', split_axis=0, concat_axis=0, tiled=True)  21.1 us
    ppermute x9, waiting for transfers between devices, shift_y(): return lax.ppermute(value, 'fsdp', pairs)  14.7 us
    ppermute x9, starting transfers between devices, shift_y(): return lax.ppermute(value, 'fsdp', pairs)  13.9 us
    pallas_call x1, Pallas kernels, attend_backward(): call(backward_kernel, 'attend_backward', kept(qkv.shape), [full(qkv), ful...  12.9 us
    ppermute x4, starting transfers between devices, swap_cfg(): return lax.ppermute(value, 'cfg', [(0, 1), (1, 0)])  9.47 us
    pallas_call x1, Pallas kernels, attend_forward(): call(forward_kernel, 'attend_forward', (kept((shards, rows, HDIM)), spill...  9.05 us
  transfers between devices with their start and end apart: 28, of which 16 were waited for; matrix products, arithmetic and copies ran while one was open for 0% of the time, Pallas kernels for 15%

profile of v2, /device:TPU:1, one launch (start us, length us, event | category | flops | bytes accessed | tf_op | source)
XLA Modules:
  0.0 192.8 jit_solution(2865635734373048390)
XLA Ops:
  2.1 9.0 %all-to-all-start.1 = ((bf16[8,16,768]{2,1,0:T(8,128)(2,1)}), bf16[8,16,768]{2,1,0:T(8,128)(2,1)S(1)}, u32[]{:S(2)}, u32[]{:S(2)}) async-start(bf16[8,16,768]{2,1,0:T(8,128)(2,1)} %spread.1), calls=%async_computation.1 | async-start | bytes 393216 | tf_op jit(solution)/shard_map/all_to_all | solution.py:514
  11.1 2.8 %pack_heads.1 = bf16[16,384,128]{2,1,0:T(8,128)(2,1)} custom-call(bf16[128,2048]{1,0:T(8,128)(2,1)} %bitcast.20, bf16[128,2048]{1,0:T(8,128)(2,1)} %bitcast.21, bf16[128,2048]{1,0:T(8,128)(2,1)} %bitcast.22), custom_call_target="tpu_custom_call" | custom-call | flops 1 | bytes 1 | tf_op jit(solution)/shard_map/pack_heads/pallas_call | solution.py:94
  13.9 6.0 %all-to-all-done.1 = bf16[8,16,768]{2,1,0:T(8,128)(2,1)S(1)} async-done(((bf16[8,16,768]{2,1,0:T(8,128)(2,1)}), bf16[8,16,768]{2,1,0:T(8,128)(2,1)S(1)}, u32[]{:S(2)}, u32[]{:S(2)}) %all-to-all-start.1) | async-done | bytes 196640 | tf_op jit(solution)/shard_map/all_to_all | solution.py:514
  20.0 4.1 %all-to-all-start = ((bf16[16,384,128]{2,1,0:T(8,128)(2,1)}), bf16[16,384,128]{2,1,0:T(8,128)(2,1)S(1)}, u32[]{:S(2)}, u32[]{:S(2)}) async-start(bf16[16,384,128]{2,1,0:T(8,128)(2,1)} %pack_heads.1), calls=%async_computation | async-start | bytes 3145728 | tf_op jit(solution)/shard_map/all_to_all | solution.py:509
  24.1 2.6 %collective-permute-start = (bf16[128,768]{1,0:T(8,128)(2,1)S(1)}, bf16[128,768]{1,0:T(8,128)(2,1)S(1)}, u32[]{:S(2)}, u32[]{:S(2)}) collective-permute-start(bf16[128,768]{1,0:T(8,128)(2,1)S(1)} %bitcast.15), channel_id=1, source_target_pairs={{0,72},{1,73},{2,74},{3,75},{4,76},{5,77},{6,78},{7,79},{8,0},{9,1... | collective-permute-start | bytes 589832 | tf_op jit(solution)/shard_map/ppermute | solution.py:458
  28.1 7.2 %collective-permute-done = bf16[128,768]{1,0:T(8,128)(2,1)S(1)} collective-permute-done((bf16[128,768]{1,0:T(8,128)(2,1)S(1)}, bf16[128,768]{1,0:T(8,128)(2,1)S(1)}, u32[]{:S(2)}, u32[]{:S(2)}) %collective-permute-start) | collective-permute-done | bytes 196640 | tf_op jit(solution)/shard_map/ppermute | solution.py:458
  38.2 4.0 %collective-permute-done.3 = bf16[128,768]{1,0:T(8,128)(2,1)S(1)} collective-permute-done((bf16[128,768]{1,0:T(8,128)(2,1)S(1)}, bf16[128,768]{1,0:T(8,128)(2,1)S(1)}, u32[]{:S(2)}, u32[]{:S(2)}) %collective-permute-start.3) | collective-permute-done | bytes 196640 | tf_op jit(solution)/shard_map/ppermute | solution.py:458
  46.9 7.8 %collective-permute-done.6.refs_3_.refs_7_ = bf16[2,128,768]{2,1,0:T(8,128)(2,1)S(1)} collective-permute-done((bf16[2,128,768]{2,1,0:T(8,128)(2,1)S(1)}, bf16[2,128,768]{2,1,0:T(8,128)(2,1)S(1)}, u32[]{:S(2)}, u32[]{:S(2)}) %collective-permute-start.6) | collective-permute-done | bytes 393248 | tf_op jit(solution)/shard_map/ppermute | solution.py:448
  54.8 5.4 %all-to-all-done.qkv_ref = bf16[16,384,128]{2,1,0:T(8,128)(2,1)S(1)} async-done(((bf16[16,384,128]{2,1,0:T(8,128)(2,1)}), bf16[16,384,128]{2,1,0:T(8,128)(2,1)S(1)}, u32[]{:S(2)}, u32[]{:S(2)}) %all-to-all-start) | async-done | bytes 1572896 | tf_op jit(solution)/shard_map/all_to_all | solution.py:509
  60.1 9.0 %attend_forward.1 = (bf16[16,128,128]{2,1,0:T(8,128)(2,1)}, bf16[2048,2048]{1,0:T(8,128)(2,1)}) custom-call(bf16[16,384,128]{2,1,0:T(8,128)(2,1)S(1)} %all-to-all-done.qkv_ref, bf16[2,128,768]{2,1,0:T(8,128)(2,1)} %copy-done.4, bf16[2,128,768]{2,1,0:T(8,128)(2,1)} %copy-done.3, bf16[2,128,768]{2,1,0:T(8,128)(2,1)} %collective-permute-done.5.refs_2_.refs_5_, ...), custom_call_target="tpu_custom_call" | custom-call | flops 1 | bytes 1 | tf_op jit(solution)/shard_map/attend_forward/pallas_call | solution.py:164
  69.2 6.4 %all-to-all-start.2 = ((bf16[16,128,128]{2,1,0:T(8,128)(2,1)}), bf16[16,128,128]{2,1,0:T(8,128)(2,1)S(1)}, u32[]{:S(2)}, u32[]{:S(2)}) async-start(bf16[16,128,128]{2,1,0:T(8,128)(2,1)} %get-tuple-element.28.mixed_ref), calls=%async_computation.2 | async-start | bytes 1048576 | tf_op jit(solution)/shard_map/all_to_all | solution.py:509
  78.5 9.9 %all-to-all-done.2.refs_8_.own_ref = bf16[16,128,128]{2,1,0:T(8,128)(2,1)S(1)} async-done(((bf16[16,128,128]{2,1,0:T(8,128)(2,1)}), bf16[16,128,128]{2,1,0:T(8,128)(2,1)S(1)}, u32[]{:S(2)}, u32[]{:S(2)}) %all-to-all-start.2) | async-done | bytes 524320 | tf_op jit(solution)/shard_map/all_to_all | solution.py:509
  88.4 3.6 %collective-permute-start.7 = (bf16[16,128,128]{2,1,0:T(8,128)(2,1)S(1)}, bf16[16,128,128]{2,1,0:T(8,128)(2,1)S(1)}, u32[]{:S(2)}, u32[]{:S(2)}) collective-permute-start(bf16[16,128,128]{2,1,0:T(8,128)(2,1)S(1)} %all-to-all-done.2.refs_8_.own_ref), channel_id=1, source_target_pairs={{0,128},{128,0},{1,129},{129,1},{2,130},{130,2},{3,131},{131,3},{4... | collective-permute-start | bytes 1572872 | tf_op jit(solution)/shard_map/ppermute | solution.py:443
  93.8 3.8 %project.1 = (bf16[128,768]{1,0:T(8,128)(2,1)}, bf16[256,768]{1,0:T(8,128)(2,1)S(1)}, f32[16,128,128]{2,1,0:T(8,128)S(1)}, bf16[16,128,128]{2,1,0:T(8,128)(2,1)S(1)}) custom-call(s32[18]{0:T(128)S(1)} %pad_add_fusion.refs_4_.place_ref, f32[2]{0:T(128)S(1)} %pad_maximum_fusion.2.refs_5_.scalar_ref, bf16[16,128,128]{2,1,0:T(8,128)(2,1)S(1)} %all-to-all-done.2.refs_8_.own_ref, ...), custom_call_target="tpu_custom_call" | custom-call | flops 1 | bytes 1 | tf_op jit(solution)/shard_map/project/pallas_call | solution.py:319
  100.4 4.6 %all-to-all-start.3 = ((bf16[16,128,128]{2,1,0:T(8,128)(2,1)}), bf16[16,128,128]{2,1,0:T(8,128)(2,1)S(1)}, u32[]{:S(2)}, u32[]{:S(2)}) async-start(bf16[16,128,128]{2,1,0:T(8,128)(2,1)} %add_after.1.order_ref), calls=%async_computation.3 | async-start | bytes 1048576 | tf_op jit(solution)/shard_map/all_to_all | solution.py:509
  105.0 2.9 %weight_gradient.1 = (bf16[4,128,768]{2,1,0:T(8,128)(2,1)}, bf16[4,128,768]{2,1,0:T(8,128)(2,1)}, bf16[4,128,768]{2,1,0:T(8,128)(2,1)}, bf16[4,128,768]{2,1,0:T(8,128)(2,1)}) custom-call(s32[18]{0:T(128)S(1)} %pad_add_fusion.refs_4_.place_ref, bf16[16,128,128]{2,1,0:T(8,128)(2,1)S(1)} %all-to-all-done.2.refs_8_.own_ref, ...), custom_call_target="tpu_custom_call" | custom-call | flops 1 | bytes 1 | tf_op jit(solution)/shard_map/weight_gradient/pallas_call | solution.py:345
  112.9 5.9 %all-to-all-done.3.grad_ref = bf16[16,128,128]{2,1,0:T(8,128)(2,1)S(1)} async-done(((bf16[16,128,128]{2,1,0:T(8,128)(2,1)}), bf16[16,128,128]{2,1,0:T(8,128)(2,1)S(1)}, u32[]{:S(2)}, u32[]{:S(2)}) %all-to-all-start.3) | async-done | bytes 524320 | tf_op jit(solution)/shard_map/all_to_all | solution.py:509
  118.8 12.9 %attend_backward.1.order_ref.refs_4_ = bf16[16,384,128]{2,1,0:T(8,128)(2,1)} custom-call(bf16[16,384,128]{2,1,0:T(8,128)(2,1)} %copy-done, bf16[16,128,128]{2,1,0:T(8,128)(2,1)} %get-tuple-element.28.mixed_ref, bf16[16,128,128]{2,1,0:T(8,128)(2,1)S(1)} %all-to-all-done.3.grad_ref, bf16[2048,2048]{1,0:T(8,128)(2,1)} %get-tuple-element.32.probs_ref, ...), custom_call_target="tpu_custom_call" | custom-call | flops 8589934592 | bytes 1 | tf_op jit(solution)/shard_map/attend_backward/pallas_call | solution.py:222
  131.7 6.8 %all-to-all-start.4 = ((bf16[16,384,128]{2,1,0:T(8,128)(2,1)}), bf16[16,384,128]{2,1,0:T(8,128)(2,1)S(1)}, u32[]{:S(2)}, u32[]{:S(2)}) async-start(bf16[16,384,128]{2,1,0:T(8,128)(2,1)} %attend_backward.1.order_ref.refs_4_), calls=%async_computation.4 | async-start | bytes 3145728 | tf_op jit(solution)/shard_map/all_to_all | solution.py:509
  139.4 6.8 %collective-permute-done.13.refs_2_ = bf16[4,128,768]{2,1,0:T(8,128)(2,1)S(1)} collective-permute-done((bf16[4,128,768]{2,1,0:T(8,128)(2,1)}, bf16[4,128,768]{2,1,0:T(8,128)(2,1)S(1)}, u32[]{:S(2)}, u32[]{:S(2)}) %collective-permute-start.13) | collective-permute-done | bytes 786464 | tf_op jit(solution)/shard_map/ppermute | solution.py:448
  147.0 2.9 %group_sums.1 = (f32[128,768]{1,0:T(8,128)}, bf16[128,768]{1,0:T(8,128)(2,1)}, bf16[128,768]{1,0:T(8,128)(2,1)}, bf16[128,768]{1,0:T(8,128)(2,1)}) custom-call(bf16[4,128,768]{2,1,0:T(8,128)(2,1)} %get-tuple-element.34.refs_0_, bf16[4,128,768]{2,1,0:T(8,128)(2,1)} %copy-done.8, bf16[4,128,768]{2,1,0:T(8,128)(2,1)} %copy-done.9, ...), custom_call_target="tpu_custom_call" | custom-call | flops 10000000000 | bytes 1 | tf_op jit(solution)/shard_map/group_sums/pallas_call | solution.py:482
  156.6 11.1 %collective-permute-done.16.refs_2_ = bf16[128,768]{1,0:T(8,128)(2,1)S(1)} collective-permute-done((bf16[128,768]{1,0:T(8,128)(2,1)}, bf16[128,768]{1,0:T(8,128)(2,1)S(1)}, u32[]{:S(2)}, u32[]{:S(2)}) %collective-permute-start.16) | collective-permute-done | bytes 196640 | tf_op jit(solution)/shard_map/ppermute | solution.py:458
  178.1 4.5 %collective-permute-start.21 = (bf16[16,768]{1,0:T(8,128)(2,1)S(1)}, bf16[16,768]{1,0:T(8,128)(2,1)S(1)}, u32[]{:S(2)}, u32[]{:S(2)}) collective-permute-start(bf16[16,768]{1,0:T(8,128)(2,1)S(1)} %get-tuple-element.50), channel_id=1, source_target_pairs={{0,4},{1,5},{2,6},{3,7},{4,0},{5,1},{6,2},{7,3},{8,12},{9,13},{10,... | collective-permute-start | bytes 73736 | tf_op jit(solution)/shard_map/ppermute | solution.py:505
  185.0 5.0 %collective-permute-start.22 = (f32[16,768]{1,0:T(8,128)S(1)}, f32[16,768]{1,0:T(8,128)S(1)}, u32[]{:S(2)}, u32[]{:S(2)}) collective-permute-start(f32[16,768]{1,0:T(8,128)S(1)} %total_of.1.own_ref), channel_id=1, source_target_pairs={{0,128},{128,0},{1,129},{129,1},{2,130},{130,2},{3,131},{131,3},{4... | collective-permute-start | bytes 147464 | tf_op jit(solution)/shard_map/ppermute | solution.py:443
  (78 shorter events, 45.7 us)
Async XLA Ops:
  2.1 17.8 %all-to-all-start.1 = ((bf16[8,16,768]{2,1,0:T(8,128)(2,1)}), bf16[8,16,768]{2,1,0:T(8,128)(2,1)S(1)}, u32[]{:S(2)}, u32[]{:S(2)}) async-start(bf16[8,16,768]{2,1,0:T(8,128)(2,1)} %spread.1), calls=%async_computation.1 | async-start | bytes 393216 | tf_op jit(solution)/shard_map/all_to_all | solution.py:514
  20.0 40.2 %all-to-all-start = ((bf16[16,384,128]{2,1,0:T(8,128)(2,1)}), bf16[16,384,128]{2,1,0:T(8,128)(2,1)S(1)}, u32[]{:S(2)}, u32[]{:S(2)}) async-start(bf16[16,384,128]{2,1,0:T(8,128)(2,1)} %pack_heads.1), calls=%async_computation | async-start | bytes 3145728 | tf_op jit(solution)/shard_map/all_to_all | solution.py:509
  24.1 11.2 %collective-permute-start = (bf16[128,768]{1,0:T(8,128)(2,1)S(1)}, bf16[128,768]{1,0:T(8,128)(2,1)S(1)}, u32[]{:S(2)}, u32[]{:S(2)}) collective-permute-start(bf16[128,768]{1,0:T(8,128)(2,1)S(1)} %bitcast.15), channel_id=1, source_target_pairs={{0,72},{1,73},{2,74},{3,75},{4,76},{5,77},{6,78},{7,79},{8,0},{9,1... | collective-permute-start | bytes 589832 | tf_op jit(solution)/shard_map/ppermute | solution.py:458
  26.7 11.5 %collective-permute-start.4 = (bf16[128,768]{1,0:T(8,128)(2,1)S(1)}, bf16[128,768]{1,0:T(8,128)(2,1)S(1)}, u32[]{:S(2)}, u32[]{:S(2)}) collective-permute-start(bf16[128,768]{1,0:T(8,128)(2,1)S(1)} %bitcast.16), channel_id=1, source_target_pairs={{0,8},{1,9},{2,10},{3,11},{4,12},{5,13},{6,14},{7,15},{8,64},{9,65... | collective-permute-start | bytes 589832 | tf_op jit(solution)/shard_map/ppermute | solution.py:458
  26.7 15.5 %collective-permute-start.3 = (bf16[128,768]{1,0:T(8,128)(2,1)S(1)}, bf16[128,768]{1,0:T(8,128)(2,1)S(1)}, u32[]{:S(2)}, u32[]{:S(2)}) collective-permute-start(bf16[128,768]{1,0:T(8,128)(2,1)S(1)} %bitcast.17), channel_id=1, source_target_pairs={{0,64},{1,65},{2,66},{3,67},{4,68},{5,69},{6,70},{7,71},{8,72},{9,... | collective-permute-start | bytes 589832 | tf_op jit(solution)/shard_map/ppermute | solution.py:458
  35.3 11.6 %collective-permute-start.2 = (bf16[2,128,768]{2,1,0:T(8,128)(2,1)S(1)}, bf16[2,128,768]{2,1,0:T(8,128)(2,1)S(1)}, u32[]{:S(2)}, u32[]{:S(2)}) collective-permute-start(bf16[2,128,768]{2,1,0:T(8,128)(2,1)S(1)} %pad_maximum_fusion.refs_0_), channel_id=1, source_target_pairs={{0,16},{16,32},{32,48},{48,0},{64,80},{80,96},{96,112},{112,64},{1... | collective-permute-start | bytes 1179656 | tf_op jit(solution)/shard_map/ppermute | solution.py:448
  36.7 10.2 %collective-permute-start.1 = (bf16[2,128,768]{2,1,0:T(8,128)(2,1)S(1)}, bf16[2,128,768]{2,1,0:T(8,128)(2,1)S(1)}, u32[]{:S(2)}, u32[]{:S(2)}) collective-permute-start(bf16[2,128,768]{2,1,0:T(8,128)(2,1)S(1)} %pad_maximum_fusion.refs_0_), channel_id=1, source_target_pairs={{0,48},{16,0},{32,16},{48,32},{64,112},{80,64},{96,80},{112,96},{1... | collective-permute-start | bytes 1179656 | tf_op jit(solution)/shard_map/ppermute | solution.py:448
  42.2 12.5 %collective-permute-start.6 = (bf16[2,128,768]{2,1,0:T(8,128)(2,1)S(1)}, bf16[2,128,768]{2,1,0:T(8,128)(2,1)S(1)}, u32[]{:S(2)}, u32[]{:S(2)}) collective-permute-start(bf16[2,128,768]{2,1,0:T(8,128)(2,1)S(1)} %pad_maximum_fusion.1.refs_4_), channel_id=1, source_target_pairs={{0,16},{16,32},{32,48},{48,0},{64,80},{80,96},{96,112},{112,64},{1... | collective-permute-start | bytes 1179656 | tf_op jit(solution)/shard_map/ppermute | solution.py:448
  43.6 11.2 %collective-permute-start.5 = (bf16[2,128,768]{2,1,0:T(8,128)(2,1)S(1)}, bf16[2,128,768]{2,1,0:T(8,128)(2,1)}, u32[]{:S(2)}, u32[]{:S(2)}) collective-permute-start(bf16[2,128,768]{2,1,0:T(8,128)(2,1)S(1)} %pad_maximum_fusion.1.refs_4_), channel_id=1, source_target_pairs={{0,48},{16,0},{32,16},{48,32},{64,112},{80,64},{96,80},{112,96},{1... | collective-permute-start | bytes 1179656 | tf_op jit(solution)/shard_map/ppermute | solution.py:448
  69.2 19.2 %all-to-all-start.2 = ((bf16[16,128,128]{2,1,0:T(8,128)(2,1)}), bf16[16,128,128]{2,1,0:T(8,128)(2,1)S(1)}, u32[]{:S(2)}, u32[]{:S(2)}) async-start(bf16[16,128,128]{2,1,0:T(8,128)(2,1)} %get-tuple-element.28.mixed_ref), calls=%async_computation.2 | async-start | bytes 1048576 | tf_op jit(solution)/shard_map/all_to_all | solution.py:509
  75.6 16.3 %collective-permute-start.8 = (bf16[2,128,768]{2,1,0:T(8,128)(2,1)}, bf16[2,128,768]{2,1,0:T(8,128)(2,1)S(1)}, u32[]{:S(2)}, u32[]{:S(2)}) collective-permute-start(bf16[2,128,768]{2,1,0:T(8,128)(2,1)} %copy-done.3), channel_id=1, source_target_pairs={{0,16},{16,32},{32,48},{48,0},{64,80},{80,96},{96,112},{112,64},{1... | collective-permute-start | bytes 1179656 | tf_op jit(solution)/shard_map/ppermute | solution.py:448
  77.0 15.0 %collective-permute-start.9 = (bf16[2,128,768]{2,1,0:T(8,128)(2,1)}, bf16[2,128,768]{2,1,0:T(8,128)(2,1)S(1)}, u32[]{:S(2)}, u32[]{:S(2)}) collective-permute-start(bf16[2,128,768]{2,1,0:T(8,128)(2,1)} %collective-permute-done.5.refs_2_.refs_5_), channel_id=1, source_target_pairs={{0,48},{16,0},{32,16},{48,32},{64,112},{80,64},{96,80},{112,96},{1... | collective-permute-start | bytes 1179656 | tf_op jit(solution)/shard_map/ppermute | solution.py:448
  100.4 18.4 %all-to-all-start.3 = ((bf16[16,128,128]{2,1,0:T(8,128)(2,1)}), bf16[16,128,128]{2,1,0:T(8,128)(2,1)S(1)}, u32[]{:S(2)}, u32[]{:S(2)}) async-start(bf16[16,128,128]{2,1,0:T(8,128)(2,1)} %add_after.1.order_ref), calls=%async_computation.3 | async-start | bytes 1048576 | tf_op jit(solution)/shard_map/all_to_all | solution.py:509
  108.0 31.4 %collective-permute-start.12 = (bf16[4,128,768]{2,1,0:T(8,128)(2,1)}, bf16[4,128,768]{2,1,0:T(8,128)(2,1)S(1)}, u32[]{:S(2)}, u32[]{:S(2)}) collective-permute-start(bf16[4,128,768]{2,1,0:T(8,128)(2,1)} %get-tuple-element.38), channel_id=1, source_target_pairs={{0,16},{16,32},{32,48},{48,0},{64,80},{80,96},{96,112},{112,64},{1... | collective-permute-start | bytes 2359304 | tf_op jit(solution)/shard_map/ppermute | solution.py:448
  109.2 36.9 %collective-permute-start.13 = (bf16[4,128,768]{2,1,0:T(8,128)(2,1)}, bf16[4,128,768]{2,1,0:T(8,128)(2,1)S(1)}, u32[]{:S(2)}, u32[]{:S(2)}) collective-permute-start(bf16[4,128,768]{2,1,0:T(8,128)(2,1)} %get-tuple-element.39), channel_id=1, source_target_pairs={{0,32},{16,48},{32,0},{48,16},{64,96},{80,112},{96,64},{112,80},{1... | collective-permute-start | bytes 2359304 | tf_op jit(solution)/shard_map/ppermute | solution.py:448
  111.9 34.3 %collective-permute-start.14 = (bf16[4,128,768]{2,1,0:T(8,128)(2,1)}, bf16[4,128,768]{2,1,0:T(8,128)(2,1)}, u32[]{:S(2)}, u32[]{:S(2)}) collective-permute-start(bf16[4,128,768]{2,1,0:T(8,128)(2,1)} %get-tuple-element.40), channel_id=1, source_target_pairs={{0,48},{16,0},{32,16},{48,32},{64,112},{80,64},{96,80},{112,96},{1... | collective-permute-start | bytes 2359304 | tf_op jit(solution)/shard_map/ppermute | solution.py:448
  131.7 58.3 %all-to-all-start.4 = ((bf16[16,384,128]{2,1,0:T(8,128)(2,1)}), bf16[16,384,128]{2,1,0:T(8,128)(2,1)S(1)}, u32[]{:S(2)}, u32[]{:S(2)}) async-start(bf16[16,384,128]{2,1,0:T(8,128)(2,1)} %attend_backward.1.order_ref.refs_4_), calls=%async_computation.4 | async-start | bytes 3145728 | tf_op jit(solution)/shard_map/all_to_all | solution.py:509
  138.5 15.6 %collective-permute-start.10 = (bf16[128,768]{1,0:T(8,128)(2,1)S(1)}, bf16[128,768]{1,0:T(8,128)(2,1)S(1)}, u32[]{:S(2)}, u32[]{:S(2)}) collective-permute-start(bf16[128,768]{1,0:T(8,128)(2,1)S(1)} %copy-done.6), channel_id=1, source_target_pairs={{0,128},{128,0},{1,129},{129,1},{2,130},{130,2},{3,131},{131,3},{4... | collective-permute-start | bytes 589832 | tf_op jit(solution)/shard_map/ppermute | solution.py:443
  149.9 6.7 %collective-permute-start.15 = (bf16[128,768]{1,0:T(8,128)(2,1)}, bf16[128,768]{1,0:T(8,128)(2,1)S(1)}, u32[]{:S(2)}, u32[]{:S(2)}) collective-permute-start(bf16[128,768]{1,0:T(8,128)(2,1)} %get-tuple-element.42), channel_id=1, source_target_pairs={{0,8},{1,9},{2,10},{3,11},{4,12},{5,13},{6,14},{7,15},{8,64},{9,65... | collective-permute-start | bytes 589832 | tf_op jit(solution)/shard_map/ppermute | solution.py:458
  151.0 16.7 %collective-permute-start.16 = (bf16[128,768]{1,0:T(8,128)(2,1)}, bf16[128,768]{1,0:T(8,128)(2,1)S(1)}, u32[]{:S(2)}, u32[]{:S(2)}) collective-permute-start(bf16[128,768]{1,0:T(8,128)(2,1)} %get-tuple-element.43), channel_id=1, source_target_pairs={{0,64},{1,65},{2,66},{3,67},{4,68},{5,69},{6,70},{7,71},{8,72},{9,... | collective-permute-start | bytes 589832 | tf_op jit(solution)/shard_map/ppermute | solution.py:458
  153.1 15.4 %collective-permute-start.17 = (bf16[128,768]{1,0:T(8,128)(2,1)}, bf16[128,768]{1,0:T(8,128)(2,1)S(1)}, u32[]{:S(2)}, u32[]{:S(2)}) collective-permute-start(bf16[128,768]{1,0:T(8,128)(2,1)} %get-tuple-element.44), channel_id=1, source_target_pairs={{0,72},{1,73},{2,74},{3,75},{4,76},{5,77},{6,78},{7,79},{8,0},{9,1... | collective-permute-start | bytes 589832 | tf_op jit(solution)/shard_map/ppermute | solution.py:458
  170.5 6.6 %collective-permute-start.18 = (bf16[2,16,768]{2,1,0:T(8,128)(2,1)S(1)}, bf16[2,16,768]{2,1,0:T(8,128)(2,1)S(1)}, u32[]{:S(2)}, u32[]{:S(2)}) collective-permute-start(bf16[2,16,768]{2,1,0:T(8,128)(2,1)S(1)} %get-tuple-element.46), channel_id=1, source_target_pairs={{0,1},{1,2},{2,3},{3,0},{4,5},{5,6},{6,7},{7,4},{8,9},{9,10},{10,1... | collective-permute-start | bytes 147464 | tf_op jit(solution)/shard_map/ppermute | solution.py:503
  178.1 6.9 %collective-permute-start.21 = (bf16[16,768]{1,0:T(8,128)(2,1)S(1)}, bf16[16,768]{1,0:T(8,128)(2,1)S(1)}, u32[]{:S(2)}, u32[]{:S(2)}) collective-permute-start(bf16[16,768]{1,0:T(8,128)(2,1)S(1)} %get-tuple-element.50), channel_id=1, source_target_pairs={{0,4},{1,5},{2,6},{3,7},{4,0},{5,1},{6,2},{7,3},{8,12},{9,13},{10,... | collective-permute-start | bytes 73736 | tf_op jit(solution)/shard_map/ppermute | solution.py:505
  185.0 6.5 %collective-permute-start.22 = (f32[16,768]{1,0:T(8,128)S(1)}, f32[16,768]{1,0:T(8,128)S(1)}, u32[]{:S(2)}, u32[]{:S(2)}) collective-permute-start(f32[16,768]{1,0:T(8,128)S(1)} %total_of.1.own_ref), channel_id=1, source_target_pairs={{0,128},{128,0},{1,129},{129,1},{2,130},{130,2},{3,131},{131,3},{4... | collective-permute-start | bytes 147464 | tf_op jit(solution)/shard_map/ppermute | solution.py:443
  (17 other events, 146.5 us)
